TPU v7x, 32 devices: a whole 2x2x4 slice. The times are simulated.
32 devices in a mesh: dp: 8 (over z, y), group: 4 (over x, core).
Axes of the slice: x: 2, y: 2, z: 4, core: 2. Of those that a mesh axis runs over, the one named last changes fastest.
Arguments:
- features: bfloat16 [2, 32, 128, 512], P(None, ('dp', 'group')), may hold values from -6 to 6
- span_starts: int32 [2, 32, 10], P(None, ('dp', 'group')), may hold values from 0 to 128, as said below
- labels: int32 [2, 32, 128], P(None, ('dp', 'group')), may hold values from 0 to 503
- feature_norm: float32 [2, 512], replicated
- feature_first: float32 [2, 512], replicated, may hold values from -1.9073486e-05 to 1.9073486e-05
- feature_second: float32 [2, 512], replicated, may hold values from 2.6034745e-12 to 1.0381954e-11
- projection: float32 [512, 768], P('dp', 'group'), may hold values from -0.25 to 0.25
- projection_first: float32 [512, 768], P('dp', 'group'), may hold values from -4.7683716e-06 to 4.7683716e-06
- projection_second: float32 [512, 768], P('dp', 'group'), may hold values from 1.6291681e-13 to 6.5166725e-13
- vectors: float32 [7, 768], replicated
- vector_first: float32 [7, 768], replicated, may hold values from -1.9073486e-05 to 1.9073486e-05
- vector_second: float32 [7, 768], replicated, may hold values from 2.6034745e-12 to 1.0381954e-11
- conv_weight: float32 [128, 48, 768], P('group', None, 'dp'), may hold values from -0.078125 to 0.078125
- conv_first: float32 [128, 48, 768], P('group', None, 'dp'), may hold values from -4.7683716e-06 to 4.7683716e-06
- conv_second: float32 [128, 48, 768], P('group', None, 'dp'), may hold values from 1.6291681e-13 to 6.5166725e-13
- head: float32 [768, 256], P('dp', 'group'), may hold values from -0.21875 to 0.21875
- head_first: float32 [768, 256], P('dp', 'group'), may hold values from -4.7683716e-06 to 4.7683716e-06
- head_second: float32 [768, 256], P('dp', 'group'), may hold values from 1.6291681e-13 to 6.5166725e-13
- clusters: float32 [504, 256], P('group', 'dp'), may hold values from -0.3 to 0.3
- cluster_first: float32 [504, 256], P('group', 'dp'), may hold values from -4.7683716e-06 to 4.7683716e-06
- cluster_second: float32 [504, 256], P('group', 'dp'), may hold values from 1.6291681e-13 to 6.5166725e-13
- blocks: float32 [12, 768, 768], P('group', 'dp'), may hold values from -0.21875 to 0.21875
- statistics: float32 [12, 2, 768, 768], P('group', None, 'dp'), as said below
Outputs:
- loss_sum: float32 [], replicated
- masked_count: float32 [], replicated
- grad_norm: float32 [], replicated
- feature_first_new: float32 [2, 512], replicated
- feature_second_new: float32 [2, 512], replicated
- feature_norm_new: float32 [2, 512], replicated
- projection_first_new: float32 [512, 768], P('dp', 'group')
- projection_second_new: float32 [512, 768], P('dp', 'group')
- projection_new: float32 [512, 768], P('dp', 'group')
- vector_first_new: float32 [7, 768], replicated
- vector_second_new: float32 [7, 768], replicated
- vectors_new: float32 [7, 768], replicated
- conv_first_new: float32 [128, 48, 768], P('group', None, 'dp')
- conv_second_new: float32 [128, 48, 768], P('group', None, 'dp')
- conv_weight_new: float32 [128, 48, 768], P('group', None, 'dp')
- head_first_new: float32 [768, 256], P('dp', 'group')
- head_second_new: float32 [768, 256], P('dp', 'group')
- head_new: float32 [768, 256], P('dp', 'group')
- cluster_first_new: float32 [504, 256], P('group', 'dp')
- cluster_second_new: float32 [504, 256], P('group', 'dp')
- clusters_new: float32 [504, 256], P('group', 'dp')
- block_grad: float32 [12, 768, 768], P('group', 'dp')
- statistics_new: float32 [12, 2, 768, 768], P('group', None, 'dp')
- blocks_new: float32 [12, 768, 768], P('group', 'dp')
Inputs may be any that keep to these rules, and one draw needn't show every extreme that they name: `span_starts`: an entry equal to 128 names no span; every other entry is at most 118; every clip has at least 3 spans. `statistics`: each left and right matrix is symmetric and positive definite.
All inputs are finite; a program needn't handle non-finite values.
Results may differ from a plain program's by a relative error of at most 0.008.
The roundings to bfloat16 on the way count: a program that leaves them out, or rounds other values in their place, can miss the bound.
Values may be sent and summed in bfloat16 or wider, within the bound.
A program may use at most 448 MiB of HBM per device.

v0:
```python
import jax
import jax.numpy as jnp
from jax import lax
from jax.sharding import PartitionSpec as P

D = 768
HEADS = 12
HEAD = 64
TAPS = 128
CLIP = 128
SPAN = 10
LAYERS = 1
MICRO = 2
NEWTON = 3
STEP = 10


HIGH = lax.Precision.HIGHEST
beta_one = 0.9
beta_two = 0.98
adam_eps = 1e-08
rate_matrix = 0.02
rate_vector = 0.5
rate_shampoo = 0.2
decay_weight = 0.01
stat_decay = 0.95
max_norm = 0.01
inv_temp = 10.0
tap_block = 16


def for_sending(array):

    def short(part):
        return part.astype(jnp.bfloat16) if part.dtype == jnp.float32 else part

    return jax.tree.map(short, array)


def spread_2(array, axis, root):
    mine = lax.axis_index(axis) == root
    return lax.psum(jnp.where(mine, array, jnp.zeros_like(array)), axis)


def to_low(values):
    return values.astype(jnp.bfloat16)


def product(spec, left, right):
    return jnp.einsum(spec, left, right, preferred_element_type=jnp.float32)


def norm_rows(values, gain, bias):
    average = jnp.mean(values, -1, keepdims=True)
    centred = values - average
    spread = jnp.mean(centred * centred, -1, keepdims=True)
    return centred * lax.rsqrt(spread + 1e-05) * gain + bias


def unit_rows(values):
    return values * lax.rsqrt(jnp.sum(values * values, -1, keepdims=True) + 1e-06)


def gelu_exact(values):
    return jax.nn.gelu(values, approximate=False)


def frame_mask(starts):
    frames = jnp.arange(CLIP, dtype=jnp.int32)[:, None]
    inside = (frames >= starts[None, :]) & (frames < starts[None, :] + SPAN)
    return jnp.any(inside, axis=1).astype(jnp.float32)


def tap_windows(padded, first, count, frames):
    return jnp.stack(
        [lax.dynamic_slice_in_dim(padded, first + offset, frames, 0) for offset in range(count)]
    )


def conv_apply(values, kernel, left):
    frames, width = values.shape
    taps, group_width = (kernel.shape[0], kernel.shape[1])
    groups = width // group_width
    block = min(tap_block, taps)
    padded = jnp.pad(values, ((left, taps - 1 - left), (0, 0)))
    shaped = kernel.reshape(taps // block, block, group_width, groups, group_width)

    def one_block(total, index):
        windows = tap_windows(padded, index * block, block, frames).reshape(
            block, frames, groups, group_width
        )
        return (total + product("tngc,tcgd->ngd", windows, shaped[index]), None)

    total, _ = lax.scan(
        one_block, jnp.zeros((frames, groups, group_width), jnp.float32), jnp.arange(taps // block)
    )
    return total.reshape(frames, width)


def conv_weight_grad(values, upstream, taps, group_width, left):
    frames, width = values.shape
    groups = width // group_width
    block = min(tap_block, taps)
    padded = jnp.pad(values, ((left, taps - 1 - left), (0, 0)))
    shaped_up = upstream.reshape(frames, groups, group_width)

    def one_block(carry, index):
        windows = tap_windows(padded, index * block, block, frames).reshape(
            block, frames, groups, group_width
        )
        return (carry, product("tngc,ngd->tcgd", windows, shaped_up))

    _, pieces = lax.scan(one_block, 0, jnp.arange(taps // block))
    return pieces.reshape(taps, group_width, width)


def inverse_root(matrix):
    size = matrix.shape[0]
    identity = jnp.eye(size, dtype=jnp.float32)
    damped = matrix + 0.0001 * (jnp.trace(matrix) / size) * identity
    magnitude = jnp.sqrt(jnp.sum(damped * damped))
    current = damped / magnitude
    result = identity * magnitude ** (-0.25)
    for sweep in range(NEWTON):
        factor = (5.0 * identity - current) * 0.25
        result = jnp.dot(result, factor, precision=HIGH)
        square = jnp.dot(factor, factor, precision=HIGH)
        current = jnp.dot(jnp.dot(square, square, precision=HIGH), current, precision=HIGH)
    return result


def adamw(weight, grad, first, second, rate, decay):
    first = beta_one * first + (1 - beta_one) * grad
    second = beta_two * second + (1 - beta_two) * grad * grad
    corrected = first / (1 - beta_one**STEP)
    scaled = jnp.sqrt(second / (1 - beta_two**STEP)) + adam_eps
    return (first, second, weight - rate * (corrected / scaled + decay * weight))


def layer_forward(hidden, weights, gains):
    frames = hidden.shape[0]
    blocks_ff = (weights.shape[0] - 4) // 2
    inputs = to_low(hidden)
    triple = to_low(product("nd,jde->nje", inputs, weights[:3]))
    heads = triple.reshape(frames, 3, HEADS, HEAD)
    scores = product("qhd,khd->hqk", heads[:, 0], heads[:, 1]) * HEAD ** (-0.5)
    total = jax.nn.logsumexp(scores, axis=-1)
    attention = to_low(jnp.exp(scores - total[..., None]))
    mixed = to_low(product("hqk,khd->qhd", attention, heads[:, 2]).reshape(frames, -1))
    before_one = hidden + product("nd,de->ne", mixed, weights[3])
    middle = norm_rows(before_one, gains[0], gains[1])
    middle_low = to_low(middle)
    expanded = product("nd,jde->nje", middle_low, weights[4 : 4 + blocks_ff])
    active = to_low(gelu_exact(expanded))
    before_two = middle + product("nje,jed->nd", active, weights[4 + blocks_ff :])
    saved = (inputs, triple, total, mixed, before_one, middle_low, expanded, active, before_two)
    return (norm_rows(before_two, gains[2], gains[3]), saved)


def layer_backward(upstream, weights, gains, saved):
    inputs, triple, total, mixed, before_one, middle_low, expanded, active, before_two = saved
    frames = inputs.shape[0]
    blocks_ff = (weights.shape[0] - 4) // 2
    _, second_back = jax.vjp(norm_rows, before_two, gains[2], gains[3])
    two_grad, gain_two, bias_two = second_back(upstream)
    reduced_grad = to_low(two_grad)
    active_grad = product("nd,jed->nje", reduced_grad, weights[4 + blocks_ff :])
    down_grad = product("nje,nd->jed", active, reduced_grad)
    _, gelu_back = jax.vjp(gelu_exact, expanded)
    expanded_grad = to_low(gelu_back(active_grad)[0])
    middle_grad = two_grad + product("nje,jde->nd", expanded_grad, weights[4 : 4 + blocks_ff])
    up_grad = product("nd,nje->jde", middle_low, expanded_grad)
    _, first_back = jax.vjp(norm_rows, before_one, gains[0], gains[1])
    one_grad, gain_one, bias_one = first_back(middle_grad)
    attended_grad = to_low(one_grad)
    mixed_grad = to_low(
        product("ne,de->nd", attended_grad, weights[3]).reshape(frames, HEADS, HEAD)
    )
    out_grad = product("nd,ne->de", mixed, attended_grad)
    heads = triple.reshape(frames, 3, HEADS, HEAD)
    query, keys, values = (heads[:, 0], heads[:, 1], heads[:, 2])
    scores = product("qhd,khd->hqk", query, keys) * HEAD ** (-0.5)
    attention_full = jnp.exp(scores - total[..., None])
    attention = to_low(attention_full)
    attention_grad = product("qhd,khd->hqk", mixed_grad, values)
    values_grad = product("hqk,qhd->khd", attention, mixed_grad)
    row_dot = jnp.sum(attention_full * attention_grad, -1, keepdims=True)
    score_grad = to_low(attention_full * (attention_grad - row_dot))
    query_grad = product("hqk,khd->qhd", score_grad, keys) * HEAD ** (-0.5)
    keys_grad = product("hqk,qhd->khd", score_grad, query) * HEAD ** (-0.5)
    triple_grad = to_low(jnp.stack([query_grad, keys_grad, values_grad], 1).reshape(frames, 3, -1))
    hidden_grad = one_grad + product("nje,jde->nd", triple_grad, weights[:3])
    triple_weight_grad = product("nd,nje->jde", inputs, triple_grad)
    weight_grads = jnp.concatenate([triple_weight_grad, out_grad[None], up_grad, down_grad], 0)
    return (hidden_grad, weight_grads, jnp.stack([gain_one, bias_one, gain_two, bias_two]))


def clip_step(weights, frames_in, mask, targets, inverse_count):
    feature_norm, projection, vectors, kernel, flipped, head, centers_low, blocks = weights
    group_width = kernel.shape[1]
    frames_full = frames_in.astype(jnp.float32)
    normed_low = to_low(norm_rows(frames_full, feature_norm[0], feature_norm[1]))
    projected = product("nf,fd->nd", normed_low, projection)
    picked = mask[:, None] > 0
    hidden = jnp.where(picked, vectors[0][None, :], projected)
    hidden_low = to_low(hidden)
    kernel_out = conv_apply(hidden_low, kernel, TAPS // 2)
    before_enc = hidden + gelu_exact(kernel_out)
    current = norm_rows(before_enc, vectors[1], vectors[2])
    level = 0
    current, saved = layer_forward(current, blocks, vectors[3 + 4 * level : 7 + 4 * level])
    kept = [saved]
    final_low = to_low(current)
    embedded = product("nd,dp->np", final_low, head)
    unit_low = to_low(unit_rows(embedded))
    logits = product("np,cp->nc", unit_low, centers_low) * inv_temp
    total = jax.nn.logsumexp(logits, axis=-1)
    choose = targets[:, None] == jnp.arange(logits.shape[1], dtype=jnp.int32)[None, :]
    target = jnp.sum(jnp.where(choose, logits, 0.0), axis=-1)
    loss = jnp.sum(mask * (total - target))
    logit_grad = to_low(
        (jnp.exp(logits - total[:, None]) - choose.astype(jnp.float32))
        * (mask * inverse_count)[:, None]
    )
    unit_grad = product("nc,cp->np", logit_grad, centers_low) * inv_temp
    center_grad = product("nc,np->cp", logit_grad, unit_low) * inv_temp
    _, unit_back = jax.vjp(unit_rows, embedded)
    embedded_grad = to_low(unit_back(unit_grad)[0])
    current_grad = product("np,dp->nd", embedded_grad, head)
    head_grad = product("nd,np->dp", final_low, embedded_grad)
    block_grads = []
    gain_grads = []
    for level in reversed(range(LAYERS)):
        current_grad, weight_grad, gain_grad = layer_backward(
            current_grad, blocks, vectors[3 + 4 * level : 7 + 4 * level], kept[level]
        )
        block_grads.insert(0, weight_grad)
        gain_grads.insert(0, gain_grad)
    _, encoder_back = jax.vjp(norm_rows, before_enc, vectors[1], vectors[2])
    encoder_grad, encoder_gain, encoder_bias = encoder_back(current_grad)
    _, gelu_back = jax.vjp(gelu_exact, kernel_out)
    kernel_out_grad = to_low(gelu_back(encoder_grad)[0])
    hidden_grad = encoder_grad + conv_apply(kernel_out_grad, flipped, TAPS // 2 - 1)
    kernel_grad = conv_weight_grad(hidden_low, kernel_out_grad, TAPS, group_width, TAPS // 2)
    embed_grad = jnp.sum(jnp.where(picked, hidden_grad, 0.0), 0)
    projected_grad = to_low(jnp.where(picked, 0.0, hidden_grad))
    normed_grad = product("nd,fd->nf", projected_grad, projection)
    projection_grad = product("nf,nd->fd", normed_low, projected_grad)
    _, feature_back = jax.vjp(norm_rows, frames_full, feature_norm[0], feature_norm[1])
    _, feature_gain, feature_bias = feature_back(normed_grad)
    vector_grad = jnp.concatenate(
        [embed_grad[None], encoder_gain[None], encoder_bias[None]] + gain_grads, 0
    )
    feature_grad = jnp.stack([feature_gain, feature_bias])
    return (
        loss,
        (
            feature_grad,
            vector_grad,
            projection_grad,
            kernel_grad,
            head_grad,
            center_grad,
            jnp.concatenate(block_grads, 0),
        ),
    )


def reduce_grads(parts):
    proj_part, kernel_part, head_part, center_part, block_part = parts
    grouped = (
        lax.psum_scatter(proj_part, "group", scatter_dimension=1, tiled=True),
        lax.psum_scatter(kernel_part, "group", scatter_dimension=0, tiled=True),
        lax.psum_scatter(head_part, "group", scatter_dimension=1, tiled=True),
        lax.psum_scatter(center_part, "group", scatter_dimension=0, tiled=True),
        lax.psum_scatter(block_part, "group", scatter_dimension=0, tiled=True),
    )
    proj_part, kernel_part, head_part, center_part, block_part = grouped
    return (
        lax.psum_scatter(proj_part, "dp", scatter_dimension=0, tiled=True),
        lax.psum_scatter(kernel_part, "dp", scatter_dimension=2, tiled=True),
        lax.psum_scatter(head_part, "dp", scatter_dimension=0, tiled=True),
        lax.psum_scatter(center_part, "dp", scatter_dimension=1, tiled=True),
        lax.psum_scatter(block_part, "dp", scatter_dimension=1, tiled=True),
    )


def body(
    features,
    span_starts,
    labels,
    feature_norm,
    feature_first,
    feature_second,
    projection,
    projection_first,
    projection_second,
    vectors,
    vector_first,
    vector_second,
    conv_weight,
    conv_first,
    conv_second,
    head,
    head_first,
    head_second,
    clusters,
    cluster_first,
    cluster_second,
    blocks,
    statistics,
):
    gathered = (
        lax.all_gather(to_low(projection), "dp", axis=0, tiled=True),
        lax.all_gather(to_low(conv_weight), "dp", axis=2, tiled=True),
        lax.all_gather(to_low(head), "dp", axis=0, tiled=True),
        lax.all_gather(to_low(clusters), "dp", axis=1, tiled=True),
        lax.all_gather(to_low(blocks), "dp", axis=1, tiled=True),
    )
    proj_part, kernel_part, head_part, center_part, block_part = gathered
    proj_w, kernel_w, head_w, clusters_w, blocks_w = (
        lax.all_gather(proj_part, "group", axis=1, tiled=True),
        lax.all_gather(kernel_part, "group", axis=0, tiled=True),
        lax.all_gather(head_part, "group", axis=1, tiled=True),
        lax.all_gather(center_part, "group", axis=0, tiled=True),
        lax.all_gather(block_part, "group", axis=0, tiled=True),
    )
    taps, group_width, width = kernel_w.shape
    groups = width // group_width
    flipped = (
        kernel_w.reshape(taps, group_width, groups, group_width)[::-1]
        .transpose(0, 3, 2, 1)
        .reshape(taps, group_width, width)
    )
    center_table = clusters_w.astype(jnp.float32)
    _, center_back = jax.vjp(unit_rows, center_table)
    centers_low = to_low(unit_rows(center_table))
    weights = (feature_norm, proj_w, vectors, kernel_w, flipped, head_w, centers_low, blocks_w)
    masks = jax.vmap(jax.vmap(frame_mask))(span_starts)
    masked_count = lax.psum(jnp.sum(masks), ("dp", "group"))
    inverse_count = 1.0 / masked_count

    def clip_scan(carry, inputs):
        loss, parts = clip_step(weights, inputs[0], inputs[1], inputs[2], inverse_count)
        return ((carry[0] + loss, jax.tree.map(jnp.add, carry[1], parts)), None)

    zeros = (
        jnp.zeros(feature_norm.shape, jnp.float32),
        jnp.zeros(vectors.shape, jnp.float32),
        jnp.zeros(proj_w.shape, jnp.float32),
        jnp.zeros(kernel_w.shape, jnp.float32),
        jnp.zeros(head_w.shape, jnp.float32),
        jnp.zeros(clusters_w.shape, jnp.float32),
        jnp.zeros(blocks_w.shape, jnp.float32),
    )
    loss_local = jnp.zeros((), jnp.float32)
    small_local = (zeros[0], zeros[1])
    large_total = ()
    for batch in range(MICRO):
        (loss_batch, parts), _ = lax.scan(
            clip_scan,
            (jnp.zeros((), jnp.float32), zeros),
            (features[batch], masks[batch], labels[batch]),
        )
        loss_local = loss_local + loss_batch
        small_local = (small_local[0] + parts[0], small_local[1] + parts[1])
        large = (parts[2], parts[3], parts[4], center_back(parts[5])[0], parts[6])
        large_total = large if batch == 0 else jax.tree.map(jnp.add, large_total, large)
    large_total = reduce_grads(large_total)
    feature_grad, vector_grad, loss_sum = lax.psum(
        (small_local[0], small_local[1], loss_local), ("dp", "group")
    )
    local_squares = sum((jnp.sum(part * part) for part in large_total))
    norm_square = (
        lax.psum(local_squares, ("dp", "group"))
        + jnp.sum(feature_grad * feature_grad)
        + jnp.sum(vector_grad * vector_grad)
    )
    grad_norm = jnp.sqrt(norm_square)
    factor = jnp.minimum(1.0, max_norm / (grad_norm + 1e-06))
    proj_grad, kernel_grad, head_grad, cluster_grad, block_rows = [
        part * factor for part in large_total
    ]
    feature_out = adamw(
        feature_norm, feature_grad * factor, feature_first, feature_second, rate_vector, 0.0
    )
    projection_out = adamw(
        projection, proj_grad, projection_first, projection_second, rate_matrix, decay_weight
    )
    vector_out = adamw(vectors, vector_grad * factor, vector_first, vector_second, rate_vector, 0.0)
    conv_out = adamw(conv_weight, kernel_grad, conv_first, conv_second, rate_matrix, decay_weight)
    head_out = adamw(head, head_grad, head_first, head_second, rate_matrix, decay_weight)
    cluster_out = adamw(
        clusters, cluster_grad, cluster_first, cluster_second, rate_matrix, decay_weight
    )
    full_blocks = lax.all_gather(block_rows.astype(jnp.bfloat16), "dp", axis=1, tiled=True).astype(
        block_rows.dtype
    )
    rows = block_rows.shape[1]
    here = lax.axis_index("dp")
    first_row = here * rows
    column_slice = lax.dynamic_slice_in_dim(full_blocks, first_row, rows, 2)
    left_rows = stat_decay * statistics[:, 0] + (1 - stat_decay) * jnp.einsum(
        "brk,bck->brc", block_rows, full_blocks, precision=HIGH
    )
    right_rows = stat_decay * statistics[:, 1] + (1 - stat_decay) * jnp.einsum(
        "bkr,bkc->brc", column_slice, full_blocks, precision=HIGH
    )
    group_blocks = block_rows.shape[0]
    dp_size = lax.axis_size("dp")
    owners = [
        (2 * member + side) * dp_size // (2 * group_blocks)
        for member in range(group_blocks)
        for side in range(2)
    ]
    left_full, right_full = (
        lax.all_gather(left_rows.astype(jnp.bfloat16), "dp", axis=1, tiled=True).astype(
            left_rows.dtype
        ),
        lax.all_gather(right_rows.astype(jnp.bfloat16), "dp", axis=1, tiled=True).astype(
            right_rows.dtype
        ),
    )
    sources = [
        left_full[member] if side == 0 else right_full[member]
        for member in range(group_blocks)
        for side in range(2)
    ]
    roots = []
    for index in range(2 * group_blocks):
        owner = owners[index]
        root = lax.cond(here == owner, inverse_root, jnp.zeros_like, sources[index])
        root = spread_2(for_sending(root), "dp", owner).astype(root.dtype)
        roots.append(root)
    stacked = jnp.stack(roots).reshape(group_blocks, 2, D, D)
    left_root_rows = lax.dynamic_slice_in_dim(stacked[:, 0], first_row, rows, 1)
    update_rows = jnp.einsum(
        "brk,bkc->brc",
        jnp.einsum("brk,bkc->brc", left_root_rows, full_blocks, precision=HIGH),
        stacked[:, 1],
        precision=HIGH,
    )
    blocks_new = blocks - rate_shampoo * (update_rows + decay_weight * blocks)
    statistics_new = jnp.stack([left_rows, right_rows], 1)
    return (
        loss_sum,
        masked_count,
        grad_norm,
        feature_out[0],
        feature_out[1],
        feature_out[2],
        projection_out[0],
        projection_out[1],
        projection_out[2],
        vector_out[0],
        vector_out[1],
        vector_out[2],
        conv_out[0],
        conv_out[1],
        conv_out[2],
        head_out[0],
        head_out[1],
        head_out[2],
        cluster_out[0],
        cluster_out[1],
        cluster_out[2],
        block_rows,
        statistics_new,
        blocks_new,
    )


def solution(mesh):
    in_specs = (
        P(None, ("dp", "group"), None, None),
        P(None, ("dp", "group"), None),
        P(None, ("dp", "group"), None),
        P(),
        P(),
        P(),
        P("dp", "group"),
        P("dp", "group"),
        P("dp", "group"),
        P(),
        P(),
        P(),
        P("group", None, "dp"),
        P("group", None, "dp"),
        P("group", None, "dp"),
        P("dp", "group"),
        P("dp", "group"),
        P("dp", "group"),
        P("group", "dp"),
        P("group", "dp"),
        P("group", "dp"),
        P("group", "dp", None),
        P("group", None, "dp", None),
    )
    out_specs = (
        P(),
        P(),
        P(),
        P(),
        P(),
        P(),
        P("dp", "group"),
        P("dp", "group"),
        P("dp", "group"),
        P(),
        P(),
        P(),
        P("group", None, "dp"),
        P("group", None, "dp"),
        P("group", None, "dp"),
        P("dp", "group"),
        P("dp", "group"),
        P("dp", "group"),
        P("group", "dp"),
        P("group", "dp"),
        P("group", "dp"),
        P("group", "dp", None),
        P("group", None, "dp", None),
        P("group", "dp", None),
    )
    return jax.shard_map(body, mesh=mesh, in_specs=in_specs, out_specs=out_specs, check_vma=False)
```

profile of v0, /device:TPU:13, one launch (start us, length us, event | category | flops | bytes accessed | tf_op | source)
XLA Modules:
  0.0 2482.6 jit_solution(17212553662631811330)
XLA Ops:
  11.5 96.5 %all-gather.10.cloned.1.call-done = bf16[32,48,768]{1,0,2:T(8,128)(2,1)} async-done(((bf16[32,48,96]{1,0,2:T(8,128)(2,1)}), bf16[32,48,768]{1,0,2:T(8,128)(2,1)}) %all-gather.10.cloned.1.call-update) | async-done | bytes 2359312 | tf_op jit(solution)/shard_map/all_gather | solution.py:315
  108.0 8.0 copy.448
  117.3 42.1 %psum.78 = f32[]{:T(128)} all-reduce(f32[]{:T(128)} %convert_reduce_fusion.2), channel_id=1, replica_groups=mesh['dp'=8,'group'=4] {'dp','group'}, use_global_device_ids=true, to_apply=%region_38.39 | all-reduce | flops 1 | bytes 8 | tf_op jit(solution)/shard_map/psum | solution.py:340
  159.5 21.8 all_gather.47
  181.5 24.7 all-gather
  206.4 24.5 all_gather.39
  231.0 25.0 %all-gather.1 = bf16[4,126,256]{2,1,0:T(8,128)(2,1)S(1)} all-gather(bf16[1,126,256]{2,1,0:T(8,128)(2,1)S(1)} %copy.460), channel_id=1, replica_groups=mesh['dp'=8,'group'=4] {'group'}, dimensions={0}, use_global_device_ids=true | all-gather | bytes 322560 | tf_op jit(solution)/shard_map/all_gather | solution.py:325
  256.7 8.7 all_gather.40
  269.4 6.6 all_gather.46
  277.2 13.3 copy.477
  290.4 30.4 %rev.3 = bf16[128,48,16,48]{0,3,2,1:T(8,128)(2,1)} reverse(bf16[128,48,16,48]{0,3,2,1:T(8,128)(2,1)} %bitcast.932), dimensions={0} | reverse | bytes 18874368 | tf_op jit(solution)/shard_map/rev | solution.py:331
  320.8 42.7 %copy.478 = bf16[128,48,16,48]{3,2,1,0:T(8,128)(2,1)} copy(bf16[128,48,16,48]{0,1,2,3:T(8,128)(2,1)} %bitcast.933) | data formatting | bytes 18874368 | tf_op jit(solution)/shard_map/transpose | solution.py:332
  363.5 32.8 %copy.480 = bf16[8,16,48,16,48]{2,4,1,3,0:T(8,128)(2,1)} copy(bf16[8,16,48,16,48]{4,3,2,1,0:T(8,128)(2,1)} %bitcast.918) | data formatting | bytes 18874368
  396.3 35.2 %reshape.1189 = bf16[8,16,48,16,48]{4,3,2,1,0:T(8,128)(2,1)} reshape(bf16[128,48,768]{2,1,0:T(8,128)(2,1)} %all-gather.12.cloned.1.call-done) | data formatting | bytes 18874368 | tf_op jit(solution)/shard_map/while/body/eval_jaxpr/reshape | solution.py:86
  431.5 32.7 %copy.449 = bf16[8,16,48,16,48]{2,4,1,3,0:T(8,128)(2,1)} copy(bf16[8,16,48,16,48]{4,3,2,1,0:T(8,128)(2,1)} %reshape.1189) | data formatting | bytes 18874368
  464.2 68.6 %while.118 = (s32[]{:T(128)}, f32[128,16,48]{0,2,1:T(8,128)S(1)}, s32[8]{0:T(128)S(1)}, bf16[8,16,48,16,48]{2,4,1,3,0:T(8,128)(2,1)}, bf16[255,768]{0,1:T(8,128)...) while((s32[]{:T(128)}, f32[128,16,48]{0,2,1:T(8,128)S(1)}, ...), condition=%wide.region_4.0_spmd.clone, body=%wide.region_3.0_spmd.clone.sunk | while | flops 151191616 | bytes 19661992 | solution.py:94
  533.3 69.2 %while.119 = (s32[]{:T(128)}, f32[128,16,48]{0,2,1:T(8,128)S(1)}, s32[8]{0:T(128)S(1)}, bf16[8,16,48,16,48]{2,4,1,3,0:T(8,128)(2,1)}, bf16[255,768]{0,1:T(8,128)...) while((s32[]{:T(128)}, f32[128,16,48]{0,2,1:T(8,128)S(1)}, ...), condition=%wide.region_22.23_spmd.clone, body=%wide.region_21.22_spmd.clone.sunk | while | flops 151191616 | bytes 19661992 | solution.py:94
  605.4 3.7 fusion.644
  624.2 3.8 fusion.540
  628.1 3.8 multiply_convert_fusion
  670.3 4.1 multiply_reduce_fusion.15
  676.8 68.6 %while.120 = (s32[]{:T(128)}, f32[128,16,48]{0,2,1:T(8,128)S(1)}, s32[8]{0:T(128)S(1)}, bf16[8,16,48,16,48]{2,4,1,3,0:T(8,128)(2,1)}, bf16[255,768]{0,1:T(8,128)...) while((s32[]{:T(128)}, f32[128,16,48]{0,2,1:T(8,128)S(1)}, ...), condition=%wide.region_48.49_spmd.clone, body=%wide.region_47.48_spmd.clone.sunk | while | flops 151191616 | bytes 19661992 | solution.py:94
  745.6 16.4 broadcast.1237.clone
  762.0 58.5 %while.116 = (s32[]{:T(128)}, f32[8,16,48,16,48]{4,2,1,3,0:T(8,128)}, s32[8]{0:T(128)S(1)}, bf16[255,768]{0,1:T(8,128)(2,1)S(1)}, bf16[128,16,48]{0,2,1:T(8,128)...) while((s32[]{:T(128)}, ...), condition=%wide.region_63.64_spmd, body=%wide.region_62.63_spmd.sunk | while | flops 150995008 | bytes 22217852 | solution.py:113
  794.8 3.7 bitcast_dynamic-update-slice_fusion.4
  820.5 68.6 %while.121 = (s32[]{:T(128)}, f32[128,16,48]{0,2,1:T(8,128)S(1)}, s32[8]{0:T(128)S(1)}, bf16[8,16,48,16,48]{2,4,1,3,0:T(8,128)(2,1)}, bf16[255,768]{0,1:T(8,128)...) while((s32[]{:T(128)}, f32[128,16,48]{0,2,1:T(8,128)S(1)}, ...), condition=%wide.region_58.59_spmd.clone, body=%wide.region_57.58_spmd.clone.sunk | while | flops 151191616 | bytes 19661992 | solution.py:94
  893.3 16.8 broadcast.1237.clone.1
  910.0 58.6 %while.117 = (s32[]{:T(128)}, f32[8,16,48,16,48]{4,2,1,3,0:T(8,128)}, s32[8]{0:T(128)S(1)}, bf16[255,768]{0,1:T(8,128)(2,1)S(1)}, bf16[128,16,48]{0,2,1:T(8,128)...) while((s32[]{:T(128)}, ...), condition=%wide.region_65.66_spmd, body=%wide.region_64.65_spmd.sunk | while | flops 150995008 | bytes 22217852 | solution.py:113
  968.6 49.5 %add.2198 = f32[8,16,48,16,48]{4,2,1,3,0:T(8,128)} add(f32[8,16,48,16,48]{4,2,1,3,0:T(8,128)} %get-tuple-element.670, f32[8,16,48,16,48]{4,2,1,3,0:T(8,128)} %get-tuple-element.671) | non-fusion elementwise | flops 4718592 | bytes 56623104 | tf_op jit(solution)/shard_map/add | solution.py:368
  1018.2 46.1 %copy.497 = f32[8,16,48,16,48]{4,3,2,1,0:T(8,128)} copy(f32[8,16,48,16,48]{4,2,1,3,0:T(8,128)} %add.2198) | data formatting | bytes 37748736 | tf_op jit(solution)/shard_map/add | solution.py:368
  1064.3 40.1 %add.2199 = f32[128,48,768]{2,1,0:T(8,128)} reshape(f32[8,16,48,16,48]{4,3,2,1,0:T(8,128)} %copy.497) | data formatting | bytes 37748736 | tf_op jit(solution)/shard_map/add | solution.py:368
  1109.3 5.4 fusion.581
  1114.8 7.3 fusion.584
  1122.2 7.1 convolution_bitcast_fusion.1
  1129.3 6.2 convolution_bitcast_fusion
  1135.5 23.5 maximum_add_fusion
  1161.2 14.8 fusion
  1176.0 4.4 collective-permute-start
  1187.1 64.4 %reduce-scatter.24.cloned.1.call-done = f32[32,48,768]{2,1,0:T(8,128)} async-done(((f32[128,48,768]{2,1,0:T(8,128)}), f32[32,48,768]{2,1,0:T(8,128)}) %reduce-scatter.24.cloned.1.call-update) | async-done | bytes 4718608 | tf_op jit(solution)/shard_map/reduce_scatter | solution.py:273
  1251.5 12.0 copy.544
  1263.5 14.7 reshape.1242
  1278.3 177.1 %reduce-scatter.28.cloned.1.call-done = f32[3,768,768]{1,2,0:T(8,128)} async-done(((f32[12,768,768]{1,2,0:T(8,128)}), f32[3,768,768]{1,2,0:T(8,128)}) %reduce-scatter.28.cloned.1.call-update) | async-done | bytes 7077904 | tf_op jit(solution)/shard_map/reduce_scatter | solution.py:276
  1455.4 11.0 copy.550
  1466.4 8.2 copy.560
  1477.7 40.3 %reduce-scatter.36.cloned.1.call-done = f32[32,126]{1,0:T(8,128)} async-done(((f32[256,126]{1,0:T(8,128)}), f32[32,126]{1,0:T(8,128)}) %reduce-scatter.36.cloned.1.call-update) | async-done | bytes 16144
  1519.4 62.7 %reduce-scatter.34.cloned.1.call-done = f32[96,64]{1,0:T(8,128)} async-done(((f32[768,64]{1,0:T(8,128)}), f32[96,64]{1,0:T(8,128)}) %reduce-scatter.34.cloned.1.call-update) | async-done | bytes 24592
  1583.5 63.7 %reduce-scatter.30.cloned.1.call-done = f32[64,192]{1,0:T(8,128)} async-done(((f32[512,192]{1,0:T(8,128)}), f32[64,192]{1,0:T(8,128)}) %reduce-scatter.30.cloned.1.call-update) | async-done | bytes 49168 | tf_op jit(solution)/shard_map/reduce_scatter | solution.py:280
  1648.8 98.7 %reduce-scatter.32.cloned.1.call-done = f32[96,1536]{1,0:T(8,128)} async-done(((f32[768,1536]{1,0:T(8,128)}), f32[96,1536]{1,0:T(8,128)}) %reduce-scatter.32.cloned.1.call-update) | async-done | bytes 589840
  1753.6 125.8 %reduce-scatter.38.cloned.1.call-done = f32[96,2304]{1,0:T(8,128)} async-done(((f32[768,2304]{1,0:T(8,128)}), f32[96,2304]{1,0:T(8,128)}) %reduce-scatter.38.cloned.1.call-update) | async-done | bytes 884752
  1883.1 40.3 %all-reduce.6 = (f32[]{:T(128)}, f32[]{:T(128)}, f32[2,512]{1,0:T(2,128)S(1)}, f32[7,768]{1,0:T(8,128)S(1)}) all-reduce(f32[]{:T(128)S(6)} %add.2190, f32[]{:T(128)S(6)} %add.2206, f32[2,512]{1,0:T(2,128)S(1)} %maximum_add_fusion.1, f32[7,768]{1,0:T(8,128)S(1)} %add.2209), channel_id=1, replica_groups=mesh['dp'=8,'group'=4] {'dp','group'}, use_global_device_ids=true, to_apply=%region_36.37 | all-reduce | flops 6402 | bytes 51216 | tf_op jit(solution)/shard_map/psum | solution.py:370
  1929.0 63.7 %all-gather.18.cloned.1.call-done = bf16[3,768,768]{2,1,0:T(8,128)(2,1)} async-done(((bf16[3,96,768]{2,1,0:T(8,128)(2,1)}), bf16[3,768,768]{2,1,0:T(8,128)(2,1)}) %all-gather.18.cloned.1.call-update) | async-done | bytes 3538960 | tf_op jit(solution)/shard_map/all_gather | solution.py:396
  1992.6 4.8 fusion.661
  1997.9 6.0 fusion.660
  2004.0 57.2 %all-gather.22.cloned.1.call-done = bf16[3,768,768]{2,1,0:T(8,128)(2,1)} async-done(((bf16[3,96,768]{2,1,0:T(8,128)(2,1)}), bf16[3,768,768]{2,1,0:T(8,128)(2,1)}) %all-gather.22.cloned.1.call-update) | async-done | bytes 3538960 | tf_op jit(solution)/shard_map/all_gather | solution.py:420
  2061.2 5.5 convert_element_type.390
  2066.7 8.9 conditional.11
  2076.6 16.1 conditional.9
  2093.8 16.6 conditional.7
  2113.8 13.8 all-gather.20.cloned.1.call-done
  2127.6 5.5 convert_element_type.387
  2133.0 9.0 conditional.10
  2143.2 16.0 conditional.6
  2160.3 11.2 conditional.8
  2187.0 277.3 %all-reduce.10.cloned.1.call-done = (bf16[1,768,768]{2,1,0:T(8,128)(2,1)}, bf16[1,768,768]{2,1,0:T(8,128)(2,1)}, bf16[1,768,768]{2,1,0:T(8,128)(2,1)}, bf16[1,76...) async-done(((bf16[1,768,768]{2,1,0:T(8,128)(2,1)}, bf16[1,768,768]{2,1,0:T(8,128)(2,1)}, bf16[1,768,768]{2,1,0:T(8,128)(2,1)}, ...) | async-done | bytes 7077904 | tf_op jit(solution)/shard_map/psum | solution.py:42
  (1607 shorter events, 420.5 us)
Async XLA Ops:
  7.2 100.8 %all-gather.10.cloned.1.call-start = ((), (), s32[]{:S(2)}) async-start(), calls=%async_computation.9 | async-start | bytes 7077888 | tf_op jit(solution)/shard_map/all_gather | solution.py:315
  10.6 266.2 %all-gather.14.cloned.1.call-start = ((), (), s32[]{:S(2)}) async-start(), calls=%async_computation.11 | async-start | bytes 3981312 | tf_op jit(solution)/shard_map/all_gather | solution.py:318
  11.5 265.7 %all-gather.12.cloned.1.call-start = ((), (), s32[]{:S(2)}) async-start(), calls=%async_computation.10 | async-start | bytes 11796480 | tf_op jit(solution)/shard_map/all_gather | solution.py:323
  116.0 43.5 %copy-start.109 = (f32[126,32]{0,1:T(8,128)S(1)}, f32[126,32]{0,1:T(8,128)}, u32[]{:S(2)}) copy-start(f32[126,32]{0,1:T(8,128)} %param.65) | copy-start | bytes 48388
  116.0 43.5 %copy-start.98 = (f32[64,192]{1,0:T(8,128)S(1)}, f32[64,192]{1,0:T(8,128)}, u32[]{:S(2)}) copy-start(f32[64,192]{1,0:T(8,128)} %param.53) | copy-start | bytes 147460
  116.0 65.5 %copy-start.101 = (f32[96,64]{0,1:T(8,128)S(1)}, f32[96,64]{0,1:T(8,128)}, u32[]{:S(2)}) copy-start(f32[96,64]{0,1:T(8,128)} %param.62) | copy-start | bytes 73732
  116.0 140.1 %copy-start.105 = (f32[7,768]{1,0:T(8,128)S(1)}, f32[7,768]{1,0:T(8,128)}, u32[]{:S(2)}) copy-start(f32[7,768]{1,0:T(8,128)} %param.56) | copy-start | bytes 64516
  116.0 140.2 %copy-start.26 = (bf16[2,1,128,512]{3,2,1,0:T(8,128)(2,1)S(1)}, bf16[2,1,128,512]{3,2,1,0:T(8,128)(2,1)}, u32[]{:S(2)}) copy-start(bf16[2,1,128,512]{3,2,1,0:T(8,128)(2,1)} %param.47) | copy-start | bytes 786436
  116.0 140.7 %copy-start.124 = (f32[2,512]{1,0:T(2,128)S(1)}, f32[2,512]{1,0:T(2,128)}, u32[]{:S(2)}) copy-start(f32[2,512]{1,0:T(2,128)} %param.50) | copy-start | bytes 12292
  116.0 493.6 %all-gather.16.cloned.1.call-start = ((), (), s32[]{:S(2)}) async-start(), calls=%async_computation.12 | async-start | bytes 17694720 | tf_op jit(solution)/shard_map/all_gather | solution.py:326
  159.5 97.1 %copy-start.172 = (f32[2,128]{1,0:T(2,128)}, f32[2,128]{1,0:T(2,128)S(1)}, u32[]{:S(2)}) copy-start(f32[2,128]{1,0:T(2,128)S(1)} %convert_element_type.328) | copy-start | bytes 3076
  256.1 20.5 copy-start.6
  256.2 365.8 %copy-start.102 = (f32[768]{0:T(1024)}, f32[768]{0:T(1024)S(1)}, u32[]{:S(2)}) copy-start(f32[768]{0:T(1024)S(1)} %get-tuple-element.1107) | copy-start | bytes 9220
  256.2 385.2 %copy-start.114 = (f32[768]{0:T(1024)}, f32[768]{0:T(1024)S(1)}, u32[]{:S(2)}) copy-start(f32[768]{0:T(1024)S(1)} %get-tuple-element.1105) | copy-start | bytes 9220
  256.2 398.8 %copy-start.106 = (f32[768]{0:T(1024)}, f32[768]{0:T(1024)S(1)}, u32[]{:S(2)}) copy-start(f32[768]{0:T(1024)S(1)} %get-tuple-element.1106) | copy-start | bytes 9220
  256.2 418.3 %copy-start.99 = (f32[768]{0:T(1024)}, f32[768]{0:T(1024)S(1)}, u32[]{:S(2)}) copy-start(f32[768]{0:T(1024)S(1)} %get-tuple-element.1108) | copy-start | bytes 9220
  256.4 10.2 copy-start.136
  256.4 11.7 copy-start.139
  256.6 10.0 copy-start.175
  256.7 9.9 copy-start.142
  256.7 11.5 copy-start.144
  256.7 11.4 copy-start.110
  256.7 11.4 copy-start.112
  266.8 9.9 copy-start.178
  276.6 368.7 %copy-start.126 = (s32[128]{0:T(128)}, s32[128]{0:T(128)S(1)}, u32[]{:S(2)}) copy-start(s32[128]{0:T(128)S(1)} %get-tuple-element.1354) | copy-start | bytes 1540
  276.8 906.1 %reduce-scatter.26.cloned.1.call-start = ((), (), s32[]{:S(2)}) async-start(), calls=%async_computation.15 | async-start | bytes 983040 | tf_op jit(solution)/shard_map/reduce_scatter | solution.py:274
  533.1 72.4 %copy-start.40 = (f32[128,768]{1,0:T(8,128)}, f32[128,768]{1,0:T(8,128)S(1)}, u32[]{:S(2)}) copy-start(f32[128,768]{1,0:T(8,128)S(1)} %copy.451) | copy-start | bytes 1179652
  533.2 72.2 %copy-start.42 = (f32[128,768]{1,0:T(8,128)}, f32[128,768]{1,0:T(8,128)S(1)}, u32[]{:S(2)}) copy-start(f32[128,768]{1,0:T(8,128)S(1)} %copy.456) | copy-start | bytes 1179652
  609.2 65.3 %copy-start.11 = (f32[128,768]{1,0:T(8,128)}, f32[128,768]{1,0:T(8,128)S(1)}, u32[]{:S(2)}) copy-start(f32[128,768]{1,0:T(8,128)S(1)} %get-tuple-element.1404) | copy-start | bytes 1179652
  609.2 65.3 %copy-start.13 = (f32[128,768]{1,0:T(8,128)}, f32[128,768]{1,0:T(8,128)S(1)}, u32[]{:S(2)}) copy-start(f32[128,768]{1,0:T(8,128)S(1)} %get-tuple-element.1220) | copy-start | bytes 1179652
  609.2 9.9 copy-start.128
  609.4 12.6 copy-start.131
  609.6 12.3 copy-start.155
  620.9 34.1 %copy-start.17 = (f32[128,768]{1,0:T(8,128)}, f32[128,768]{1,0:T(8,128)S(1)}, u32[]{:S(2)}) copy-start(f32[128,768]{1,0:T(8,128)S(1)} %get-tuple-element.1366) | copy-start | bytes 1179652
  621.0 34.1 %copy-start.153 = (f32[128]{0:T(128)}, f32[128]{0:T(128)S(1)}, u32[]{:S(2)}) copy-start(f32[128]{0:T(128)S(1)} %broadcast_multiply_fusion.7) | copy-start | bytes 1540
  621.2 33.9 %copy-start.183 = (f32[128]{0:T(128)}, f32[128]{0:T(128)S(1)}, u32[]{:S(2)}) copy-start(f32[128]{0:T(128)S(1)} %fusion.600) | copy-start | bytes 1540
  621.7 14.7 slice-start.12
  624.0 31.1 %copy-start.19 = (f32[128,768]{1,0:T(8,128)}, f32[128,768]{1,0:T(8,128)S(1)}, u32[]{:S(2)}) copy-start(f32[128,768]{1,0:T(8,128)S(1)} %get-tuple-element.1379) | copy-start | bytes 1179652
  624.0 31.1 %copy-start.158 = (f32[128]{0:T(128)}, f32[128]{0:T(128)S(1)}, u32[]{:S(2)}) copy-start(f32[128]{0:T(128)S(1)} %broadcast_multiply_fusion.10) | copy-start | bytes 1540
  624.2 30.9 %copy-start.185 = (f32[128]{0:T(128)}, f32[128]{0:T(128)S(1)}, u32[]{:S(2)}) copy-start(f32[128]{0:T(128)S(1)} %fusion.597) | copy-start | bytes 1540
  624.2 12.2 slice-start.13
  624.2 12.2 slice-start.14
  636.0 9.6 copy-start.48
  655.5 11.1 copy-start.35
  655.5 11.1 copy-start.189
  659.1 11.1 copy-start.191
  664.5 520.3 %reduce-scatter.22.cloned.1.call-start = ((), (), s32[]{:S(2)}) async-start(), calls=%async_computation.13 | async-start | bytes 1966080 | tf_op jit(solution)/shard_map/reduce_scatter | solution.py:272
  762.0 58.5 %copy-start.4 = (f32[128,16,48]{0,2,1:T(8,128)S(1)}, f32[128,16,48]{0,2,1:T(8,128)}, u32[]{:S(2)}) copy-start(f32[128,16,48]{0,2,1:T(8,128)} %custom-call.3) | copy-start | bytes 1179652
  820.5 69.1 %copy-start.145 = (pred[128]{0:T(512)(128)(4,1)S(1)}, pred[128]{0:T(512)(128)(4,1)}, u32[]{:S(2)}) copy-start(pred[128]{0:T(512)(128)(4,1)} %copy-done.144) | copy-start | bytes 388
  893.2 358.3 %reduce-scatter.24.cloned.1.call-start = ((), (), s32[]{:S(2)}) async-start(), calls=%async_computation.14 | async-start | bytes 23592960 | tf_op jit(solution)/shard_map/reduce_scatter | solution.py:273
  893.3 16.8 copy-start.1
  1104.5 350.9 %reduce-scatter.28.cloned.1.call-start = ((), (), s32[]{:S(2)}) async-start(), calls=%async_computation.16 | async-start | bytes 35389440 | tf_op jit(solution)/shard_map/reduce_scatter | solution.py:276
  1159.2 358.8 %reduce-scatter.36.cloned.1.call-start = ((), (), s32[]{:S(2)}) async-start(), calls=%async_computation.23 | async-start | bytes 147456
  1160.4 20.0 copy-start.202
  1176.0 5.6 collective-permute-start
  1182.8 399.2 %reduce-scatter.34.cloned.1.call-start = ((), (), s32[]{:S(2)}) async-start(), calls=%async_computation.22 | async-start | bytes 442368
  1184.7 462.5 %reduce-scatter.30.cloned.1.call-start = ((), (), s32[]{:S(2)}) async-start(), calls=%async_computation.20 | async-start | bytes 589824 | tf_op jit(solution)/shard_map/reduce_scatter | solution.py:280
  1186.8 560.6 %reduce-scatter.32.cloned.1.call-start = ((), (), s32[]{:S(2)}) async-start(), calls=%async_computation.21 | async-start | bytes 5308416
  1278.2 601.1 %reduce-scatter.38.cloned.1.call-start = ((), (), s32[]{:S(2)}) async-start(), calls=%async_computation.24 | async-start | bytes 7962624
  1474.8 517.8 %all-gather.18.cloned.1.call-start = ((), (), s32[]{:S(2)}) async-start(), calls=%async_computation.17 | async-start | bytes 3981312 | tf_op jit(solution)/shard_map/all_gather | solution.py:396
  1750.2 130.8 %copy-start.15 = (f32[32,48,96]{2,1,0:T(8,128)}, f32[32,48,96]{2,1,0:T(8,128)S(1)}, u32[]{:S(2)}) copy-start(f32[32,48,96]{2,1,0:T(8,128)S(1)} %copy.545) | copy-start | bytes 1769476
  1928.9 132.3 %all-gather.22.cloned.1.call-start = ((), (), s32[]{:S(2)}) async-start(), calls=%async_computation.19 | async-start | bytes 3981312 | tf_op jit(solution)/shard_map/all_gather | solution.py:420
  1997.4 130.2 %all-gather.20.cloned.1.call-start = ((), (), s32[]{:S(2)}) async-start(), calls=%async_computation.18 | async-start | bytes 3981312 | tf_op jit(solution)/shard_map/all_gather | solution.py:417
  2004.0 460.4 %all-reduce.10.cloned.1.call-start = ((), (), s32[]{:S(2)}) async-start(), calls=%async_computation.25 | async-start | bytes 14155776 | tf_op jit(solution)/shard_map/psum | solution.py:42
  (161 other events, 450.0 us)
Sparse Core Ops, SparseCore 0:
  10.8 97.1 all-gather.9
  110.8 65.2 all-gather.13
  177.6 65.7 all-gather.11
  276.9 94.5 all-gather.15
  664.6 26.4 reduce-scatter.25
  893.3 31.3 reduce-scatter.21
  1104.6 146.8 reduce-scatter.23
  1254.3 201.0 reduce-scatter.27
  1459.3 58.5 reduce-scatter.35
  1521.6 60.3 reduce-scatter.33
  1586.0 61.2 reduce-scatter.29
  1651.1 96.2 reduce-scatter.31
  1751.6 127.6 reduce-scatter.37
  1929.0 63.5 all-gather.17
  1997.5 63.6 all-gather.21
  2063.9 63.6 all-gather.19
  2172.8 291.4 all-reduce.9
where the time goes:
time: 2500 us; the launch traced here: 2480 us
  waiting for transfers between devices  1140 us (46%)
  local copies, waits for them, and re-layouts  541 us (22%)
  matrix products  248 us (10%)
  blocking collectives  209 us (8%)
  loops' own time  181 us (7%)
  other arithmetic  129 us (5%)
  between operations  26.8 us (1%)
    unnamed x22, waiting for transfers between devices  328 us
    psum x1, waiting for transfers between devices, spread_2(): return lax.psum(jnp.where(mine, array, jnp.zeros_like(array)), axis)  277 us
    dot_general x102, matrix products, product(): return jnp.einsum(spec, left, right, preferred_element_type=jnp.float32)  234 us
    reduce_scatter x1, waiting for transfers between devices, reduce_grads(): lax.psum_scatter(block_part, 'group', scatter_dimension=0, tiled=True)  177 us
    unnamed x447, local copies, waits for them, and re-layouts  142 us
    all_gather x1, waiting for transfers between devices, body(): lax.all_gather(to_low(conv_weight), 'dp', axis=2, tiled=True)  96.5 us
    another operation x4, loops' own time, conv_apply(): lax.scan(one_block, jnp.zeros((frames, groups, group_width), jnp.float32)...  90.3 us
    dynamic_slice x48, local copies, waits for them, and re-layouts, tap_windows(): lax.dynamic_slice_in_dim(padded, first + offset, frames, 0)  88 us
  transfers between devices with their start and end apart: 18, of which 12 were waited for; matrix products, arithmetic and copies ran while one was open for 34% of the time, Pallas kernels for 0%

commit v1 on v0

v1 whole, which is shorter than its diff:
```python
import functools

import jax
import jax.numpy as jnp
from jax import lax
from jax.experimental import pallas as pl
from jax.experimental.pallas import tpu as pltpu
from jax.sharding import PartitionSpec as P

D = 768
HEADS = 12
HEAD = 64
TAPS = 128
CLIP = 128
SPAN = 10
NEWTON = 3
STEP = 10


HIGH = lax.Precision.HIGHEST
beta_one = 0.9
beta_two = 0.98
adam_eps = 1e-08
rate_matrix = 0.02
rate_vector = 0.5
rate_shampoo = 0.2
decay_weight = 0.01
stat_decay = 0.95
max_norm = 0.01
inv_temp = 10.0
STRIDE = 4


def for_sending(array):

    def short(part):
        return part.astype(jnp.bfloat16) if part.dtype == jnp.float32 else part

    return jax.tree.map(short, array)


def spread_2(array, axis, root):
    mine = lax.axis_index(axis) == root
    return lax.psum(jnp.where(mine, array, jnp.zeros_like(array)), axis)


def to_low(values):
    return values.astype(jnp.bfloat16)


def product(spec, left, right):
    return jnp.einsum(spec, left, right, preferred_element_type=jnp.float32)


def unit_rows(values):
    return values * lax.rsqrt(jnp.sum(values * values, -1, keepdims=True) + 1e-06)


def frame_mask(starts):
    frames = jnp.arange(CLIP, dtype=jnp.int32)[:, None]
    inside = (frames >= starts[None, :]) & (frames < starts[None, :] + SPAN)
    return jnp.any(inside, axis=1).astype(jnp.float32)


def inverse_root(matrix):
    size = matrix.shape[0]
    identity = jnp.eye(size, dtype=jnp.float32)
    damped = matrix + 0.0001 * (jnp.trace(matrix) / size) * identity
    magnitude = jnp.sqrt(jnp.sum(damped * damped))
    current = damped / magnitude
    result = identity * magnitude ** (-0.25)
    for sweep in range(NEWTON):
        factor = (5.0 * identity - current) * 0.25
        result = jnp.dot(result, factor, precision=HIGH)
        square = jnp.dot(factor, factor, precision=HIGH)
        current = jnp.dot(jnp.dot(square, square, precision=HIGH), current, precision=HIGH)
    return result


def adamw(weight, grad, first, second, rate, decay):
    first = beta_one * first + (1 - beta_one) * grad
    second = beta_two * second + (1 - beta_two) * grad * grad
    corrected = first / (1 - beta_one**STEP)
    scaled = jnp.sqrt(second / (1 - beta_two**STEP)) + adam_eps
    return (first, second, weight - rate * (corrected / scaled + decay * weight))


def reduce_grads(parts):
    proj_part, kernel_part, head_part, center_part, block_part = parts
    grouped = (
        lax.psum_scatter(proj_part, "group", scatter_dimension=1, tiled=True),
        lax.psum_scatter(kernel_part, "group", scatter_dimension=0, tiled=True),
        lax.psum_scatter(head_part, "group", scatter_dimension=1, tiled=True),
        lax.psum_scatter(center_part, "group", scatter_dimension=0, tiled=True),
        lax.psum_scatter(block_part, "group", scatter_dimension=0, tiled=True),
    )
    proj_part, kernel_part, head_part, center_part, block_part = grouped
    return (
        lax.psum_scatter(proj_part, "dp", scatter_dimension=0, tiled=True),
        lax.psum_scatter(kernel_part, "dp", scatter_dimension=2, tiled=True),
        lax.psum_scatter(head_part, "dp", scatter_dimension=0, tiled=True),
        lax.psum_scatter(center_part, "dp", scatter_dimension=1, tiled=True),
        lax.psum_scatter(block_part, "dp", scatter_dimension=1, tiled=True),
    )


def gather_plain(projection, conv_weight, head, clusters, blocks):
    gathered = (
        lax.all_gather(to_low(projection), "dp", axis=0, tiled=True),
        lax.all_gather(to_low(conv_weight), "dp", axis=2, tiled=True),
        lax.all_gather(to_low(head), "dp", axis=0, tiled=True),
        lax.all_gather(to_low(clusters), "dp", axis=1, tiled=True),
        lax.all_gather(to_low(blocks), "dp", axis=1, tiled=True),
    )
    proj_part, kernel_part, head_part, center_part, block_part = gathered
    return (
        lax.all_gather(proj_part, "group", axis=1, tiled=True),
        lax.all_gather(kernel_part, "group", axis=0, tiled=True),
        lax.all_gather(head_part, "group", axis=1, tiled=True),
        lax.all_gather(center_part, "group", axis=0, tiled=True),
        lax.all_gather(block_part, "group", axis=0, tiled=True),
    )


def shampoo_plain(block_rows, statistics):
    full_blocks = lax.all_gather(block_rows.astype(jnp.bfloat16), "dp", axis=1, tiled=True).astype(
        block_rows.dtype
    )
    rows = block_rows.shape[1]
    here = lax.axis_index("dp")
    first_row = here * rows
    column_slice = lax.dynamic_slice_in_dim(full_blocks, first_row, rows, 2)
    left_rows = stat_decay * statistics[:, 0] + (1 - stat_decay) * jnp.einsum(
        "brk,bck->brc", block_rows, full_blocks, precision=HIGH
    )
    right_rows = stat_decay * statistics[:, 1] + (1 - stat_decay) * jnp.einsum(
        "bkr,bkc->brc", column_slice, full_blocks, precision=HIGH
    )
    group_blocks = block_rows.shape[0]
    dp_size = lax.axis_size("dp")
    owners = [
        (2 * member + side) * dp_size // (2 * group_blocks)
        for member in range(group_blocks)
        for side in range(2)
    ]
    left_full, right_full = (
        lax.all_gather(left_rows.astype(jnp.bfloat16), "dp", axis=1, tiled=True).astype(
            left_rows.dtype
        ),
        lax.all_gather(right_rows.astype(jnp.bfloat16), "dp", axis=1, tiled=True).astype(
            right_rows.dtype
        ),
    )
    sources = [
        left_full[member] if side == 0 else right_full[member]
        for member in range(group_blocks)
        for side in range(2)
    ]
    roots = []
    for index in range(2 * group_blocks):
        owner = owners[index]
        root = lax.cond(here == owner, inverse_root, jnp.zeros_like, sources[index])
        root = spread_2(for_sending(root), "dp", owner).astype(root.dtype)
        roots.append(root)
    stacked = jnp.stack(roots).reshape(group_blocks, 2, D, D)
    left_root_rows = lax.dynamic_slice_in_dim(stacked[:, 0], first_row, rows, 1)
    update_rows = jnp.einsum(
        "brk,bkc->brc",
        jnp.einsum("brk,bkc->brc", left_root_rows, full_blocks, precision=HIGH),
        stacked[:, 1],
        precision=HIGH,
    )
    return jnp.stack([left_rows, right_rows], 1), update_rows


MESH = pl.DeviceIdType.MESH
HBM = pl.BlockSpec(memory_space=pltpu.HBM)
VMEM = pl.BlockSpec(memory_space=pltpu.VMEM)
VMEM_LIMIT = 60 * 1024 * 1024


class Place:
    def __init__(self, dp_size, group_size):
        self.dp_size, self.group_size = dp_size, group_size
        self.lines = dp_size // 2
        self.dp, self.group = lax.axis_index("dp"), lax.axis_index("group")
        self.z, self.y = self.dp // 2, self.dp % 2
        self.x, self.core = self.group // 2, self.group % 2

    def at(self, z, flip_y=0, flip_x=0, flip_core=0):
        y = self.y + flip_y * (1 - 2 * self.y)
        x = self.x + flip_x * (1 - 2 * self.x)
        core = self.core + flip_core * (1 - 2 * self.core)
        return (z * 2 + y, x * 2 + core)

    def near(self, z, p, q):
        return self.at(z, p * (1 - self.core) + q * self.core, q * (1 - self.core) + p * self.core)

    def across(self, z, p, q):
        return self.at(z, p * self.core + q * (1 - self.core), q * self.core + p * (1 - self.core), 1)


def greet(place):
    barrier = pltpu.get_barrier_semaphore()
    first = place.x * 2
    for other in range(place.dp_size):
        for core in range(2):

            @pl.when((place.dp != other) | (place.core != core))
            def _():
                pl.semaphore_signal(
                    barrier, inc=1, device_id=(other, first + core), device_id_type=MESH
                )

    for core in range(2):
        pl.semaphore_signal(
            barrier,
            inc=1,
            device_id=(place.dp, (1 - place.x) * 2 + core),
            device_id_type=MESH,
        )
    pl.semaphore_wait(barrier, 2 * place.dp_size - 1 + 2)


def guarded(condition, action):
    if condition is None:
        action()
    else:
        pl.when(condition)(action)


def both(one, two):
    if one is None:
        return two
    if two is None:
        return one
    return one & two


def piece_at(kind, ref, dp, group, shape):
    if kind == "blocks":
        start = pl.multiple_of(dp * shape[1], shape[1])
        return ref.at[pl.ds(group * shape[0], shape[0]), pl.ds(start, shape[1])]
    if kind == "conv":
        return ref.at[group, pl.ds(dp * shape[0], shape[0])]
    return ref.at[dp, group]


KINDS = ("conv", "small", "blocks")


def gather_kernel(sizes, shapes, *refs):
    place = Place(*sizes)
    count = len(KINDS)
    ins, stats_in = refs[:count], refs[count]
    outs, stats_out = refs[count + 1 : 2 * count + 1], refs[2 * count + 1]
    send_sem, recv_sem, own_sem, stat_send, stat_recv, stat_own = refs[2 * count + 2 :]
    z, last = place.z, place.lines - 1
    me = (place.dp, place.group)
    greet(place)
    sent = []
    slots = [0] * count

    def view(k, source):
        return piece_at(KINDS[k], outs[k], source[0], source[1], shapes[k])

    def identity(source):
        return source[0] * place.group_size + source[1]

    def copy_of(k, source, target, slot, own=False):
        spot = view(k, source)
        return pltpu.make_async_remote_copy(
            src_ref=ins[k] if own else spot,
            dst_ref=spot,
            send_sem=send_sem.at[k, slot],
            recv_sem=recv_sem.at[k, identity(source)],
            device_id=target,
            device_id_type=MESH,
        )

    def send(k, source, target, condition=None, own=False):
        slot = slots[k]
        slots[k] += 1
        guarded(condition, lambda: copy_of(k, source, target, slot, own).start())
        sent.append((k, source, target, slot, condition, own))

    def arrive(k, source, condition=None):
        guarded(condition, lambda: copy_of(k, source, me, 0).wait_recv())

    links = {
        "left": (place.at(z - 1), z > 0),
        "right": (place.at(z + 1), z < last),
        "p": (place.near(z, 1, 0), None),
        "q": (place.near(z, 0, 1), None),
        "core": (place.at(z, 0, 0, 1), None),
    }

    def forward(k, source, ways, condition=None, own=False):
        for way in ways:
            target, open_way = links[way]
            send(k, source, target, both(condition, open_way), own)

    def spots(offset):
        if offset == 0:
            return [(z, None, ("left", "right"))]
        return [
            (z - offset, z >= offset, ("right",)),
            (z + offset, z + offset <= last, ("left",)),
        ]

    def take(k, source, condition, ways):
        arrive(k, source, condition)
        forward(k, source, ways, condition)

    steps = place.lines + 3

    def step_z_first(k, step):
        if step == 0:
            forward(k, me, ("left", "right", "q", "p", "core"), own=True)
            return
        if step < place.lines:
            for spot, there, ways in spots(step):
                take(k, place.near(spot, 0, 0), there, ways + ("q", "p", "core"))
        if 0 <= step - 1 < place.lines:
            for spot, there, _ in spots(step - 1):
                take(k, place.near(spot, 1, 0), there, ("q", "core"))
                take(k, place.near(spot, 0, 1), there, ("core",))
        if 0 <= step - 2 < place.lines:
            for spot, there, _ in spots(step - 2):
                take(k, place.near(spot, 1, 1), there, ("core",))

    def step_z_second(k, step):
        if step == 0:
            forward(k, me, ("q", "left", "right", "p", "core"), own=True)
            return
        if step == 1:
            take(k, place.near(z, 0, 1), None, ("left", "right", "p", "core"))
        if step < place.lines:
            for spot, there, ways in spots(step):
                take(k, place.near(spot, 0, 0), there, ways + ("p", "core"))
        if 1 <= step - 1 < place.lines:
            for spot, there, ways in spots(step - 1):
                take(k, place.near(spot, 0, 1), there, ways + ("p", "core"))
        if 0 <= step - 1 < place.lines:
            for spot, there, _ in spots(step - 1):
                take(k, place.near(spot, 1, 0), there, ("core",))
        if 0 <= step - 2 < place.lines:
            for spot, there, _ in spots(step - 2):
                take(k, place.near(spot, 1, 1), there, ("core",))

    members = shapes[KINDS.index("blocks")][0]
    rows = shapes[KINDS.index("blocks")][1]

    def stat_copy(member, side):
        owner = place.core * members + member
        start = pl.multiple_of(place.dp * rows, rows)
        return owner, pltpu.make_async_remote_copy(
            src_ref=stats_in.at[member, side],
            dst_ref=stats_out.at[pl.ds(start, rows)],
            send_sem=stat_send.at[member, side],
            recv_sem=stat_recv.at[place.dp],
            device_id=(owner, place.x * 2 + side),
            device_id_type=MESH,
        )

    def stat_local(member, side):
        start = pl.multiple_of(place.dp * rows, rows)
        return pltpu.make_async_copy(
            stats_in.at[member, side], stats_out.at[pl.ds(start, rows)], stat_own
        )

    def each_stat(remote, local):
        for member in range(members):
            for side in range(2):
                owner = place.core * members + member
                mine = (place.dp == owner) & (place.core == side)
                pl.when(jnp.logical_not(mine))(lambda m=member, s=side: remote(m, s))
                pl.when(mine)(lambda m=member, s=side: local(m, s))

    own_copies = [
        pltpu.make_async_copy(ins[k], view(k, me), own_sem.at[k]) for k in range(count)
    ]
    for step in range(steps):
        for k, kind in enumerate(KINDS):
            if kind == "blocks":
                step_z_second(k, step)
            else:
                step_z_first(k, step)
        if step == 0:
            for own in own_copies:
                own.start()
        if step == 1:
            each_stat(
                lambda m, s: stat_copy(m, s)[1].start(), lambda m, s: stat_local(m, s).start()
            )
    for k in range(count):
        for spot in range(place.lines):
            for p in range(2):
                for q in range(2):
                    arrive(k, place.across(spot, p, q))
    for own in own_copies:
        own.wait()
    each_stat(lambda m, s: stat_copy(m, s)[1].wait_send(), lambda m, s: stat_local(m, s).wait())
    owned_group = place.x * 2 + place.dp // members

    @pl.when(place.dp < 2 * members)
    def _():
        for other in range(place.dp_size):

            @pl.when((place.dp != other) | (place.group != owned_group))
            def _():
                pltpu.make_async_remote_copy(
                    src_ref=stats_in.at[0, 0],
                    dst_ref=stats_out.at[pl.ds(other * rows, rows)],
                    send_sem=stat_send.at[0, 0],
                    recv_sem=stat_recv.at[other],
                    device_id=me,
                    device_id_type=MESH,
                ).wait_recv()

    for k, source, target, slot, condition, own in sent:
        guarded(
            condition,
            lambda k=k, source=source, target=target, slot=slot, own=own: copy_of(
                k, source, target, slot, own
            ).wait_send(),
        )


def full_shapes(sizes, shapes):
    dp_size, group_size = sizes
    conv, small, blocks = shapes
    return [
        (group_size, dp_size * conv[0]) + conv[1:],
        (dp_size, group_size) + small,
        (group_size * blocks[0], dp_size * blocks[1], blocks[2]),
    ]


def gather_weights(sizes, pieces, stats_low):
    shapes = [piece.shape for piece in pieces]
    outs = [
        jax.ShapeDtypeStruct(shape, jnp.bfloat16) for shape in full_shapes(sizes, shapes)
    ] + [jax.ShapeDtypeStruct((D, D), jnp.bfloat16)]
    count, devices = len(pieces), sizes[0] * sizes[1]
    members = shapes[-1][0]
    return pl.pallas_call(
        functools.partial(gather_kernel, sizes, shapes),
        out_shape=outs,
        in_specs=[HBM] * (count + 1),
        out_specs=[HBM] * (count + 1),
        scratch_shapes=[
            pltpu.SemaphoreType.DMA((count, 3 * devices)),
            pltpu.SemaphoreType.DMA((count, devices)),
            pltpu.SemaphoreType.DMA((count,)),
            pltpu.SemaphoreType.DMA((members, 2)),
            pltpu.SemaphoreType.DMA((sizes[0],)),
            pltpu.SemaphoreType.DMA,
        ],
        name="gather_weights",
        compiler_params=pltpu.CompilerParams(
            collective_id=0, has_side_effects=True, vmem_limit_bytes=16 * 1024 * 1024
        ),
    )(*pieces, stats_low)


def reduce_kernel(sizes, shapes, *refs):
    place = Place(*sizes)
    count = len(KINDS)
    refs = list(refs)

    def pull(number):
        taken = refs[:number]
        del refs[:number]
        return taken

    ins, (small_in,) = pull(count), pull(1)
    outs, (small_out, square_out, whole_out) = pull(count), pull(3)
    held, crossed, first_in, second_in, from_left, from_right = (pull(count) for _ in range(6))
    (group_box, dp_box, rows_low, whole_box) = pull(4)
    (load_sem, cross_send, cross_recv, first_send, first_recv) = pull(5)
    (second_send, second_recv, left_send, left_recv, right_send, right_recv) = pull(6)
    (group_send, group_recv, dp_send, dp_recv, row_send, row_recv, pair_send, pair_recv) = pull(8)
    z, lines, last = place.z, place.lines, place.lines - 1
    me = (place.dp, place.group)
    p_mate, q_mate, c_mate = place.near(z, 1, 0), place.near(z, 0, 1), place.at(z, 0, 0, 1)
    left, right = place.at(z - 1), place.at(z + 1)
    greet(place)

    def remote(source, target, send, recv, device):
        return pltpu.make_async_remote_copy(
            src_ref=source,
            dst_ref=target,
            send_sem=send,
            recv_sem=recv,
            device_id=device,
            device_id_type=MESH,
        )

    def f32(ref, at):
        return ref[at].astype(jnp.float32)

    z_first = [kind != "blocks" for kind in KINDS]

    def order(k):
        if z_first[k]:
            return [(p, q) for q in (1, 0) for p in (1, 0)]
        return [(p, q) for p in (1, 0) for q in (1, 0)]

    def load_of(k, p, q, spot):
        dp, group = place.near(spot, p, q)
        return pltpu.make_async_copy(
            piece_at(KINDS[k], ins[k], dp, group, shapes[k]),
            held[k].at[p, q, spot],
            load_sem.at[k, p, q, spot],
        )

    def cross_of(k, p, q, spot):
        dp, group = place.across(spot, p, q)
        return remote(
            piece_at(KINDS[k], ins[k], dp, group, shapes[k]),
            crossed[k].at[p, q, spot],
            cross_send.at[k, p, q, spot],
            cross_recv.at[k, p, q, spot],
            c_mate,
        )

    sequence = (KINDS.index("blocks"), KINDS.index("small"), KINDS.index("conv"))
    for turn in range(4):
        for k in sequence:
            p, q = order(k)[turn]

            def start_one(spot, _, k=k, p=p, q=q):
                cross_of(k, p, q, spot).start()
                load_of(k, p, q, spot).start()
                return 0

            lax.fori_loop(0, lines, start_one, 0)

    def group_copy(other):
        return remote(
            small_in, group_box.at[place.group], group_send.at[other], group_recv.at[place.group], (place.dp, other)
        )

    def each_other(size, mine, action):
        for other in range(size):
            pl.when(mine != other)(functools.partial(action, other))

    each_other(place.group_size, place.group, lambda other: group_copy(other).start())
    group_box[place.group] = small_in[...]

    def first_ready(k, p, q, spot):
        load_of(k, p, q, spot).wait()
        cross_of(k, p, q, spot).wait_recv()

    def first_out(k, a, spot):
        source = held[k].at[a, 1, spot] if z_first[k] else held[k].at[1, a, spot]
        return remote(
            source,
            first_in[k].at[a, spot],
            first_send.at[k, a, spot],
            first_recv.at[k, a, spot],
            q_mate if z_first[k] else p_mate,
        )

    def stage_one(k):
        for a in (1, 0):

            def one(spot, _, a=a):
                p, q = (a, 1) if z_first[k] else (1, a)
                first_ready(k, p, q, spot)
                total = f32(held[k], (p, q, spot)) + f32(crossed[k], (p, q, spot))
                held[k][p, q, spot] = total.astype(jnp.bfloat16)
                first_out(k, a, spot).start()
                return 0

            lax.fori_loop(0, lines, one, 0)

    for k in sequence:
        stage_one(k)

    def dp_copy(other):
        return remote(
            dp_box.at[place.dp], dp_box.at[place.dp], dp_send.at[other], dp_recv.at[place.dp], (other, place.group)
        )

    def group_wait(other):
        group_copy(other).wait_send()
        remote(small_in, group_box.at[other], group_send.at[other], group_recv.at[other], me).wait_recv()

    each_other(place.group_size, place.group, group_wait)
    total = group_box[0]
    for other in range(1, place.group_size):
        total = total + group_box[other]
    dp_box[place.dp] = total
    each_other(place.dp_size, place.dp, lambda other: dp_copy(other).start())

    def second_out(k, spot):
        return remote(
            held[k].at[1, 0, spot],
            second_in[k].at[spot],
            second_send.at[k, spot],
            second_recv.at[k, spot],
            p_mate,
        )

    def gathered_sum(k, p, q, spot):
        first_ready(k, p, q, spot)
        a = p if z_first[k] else q
        first_out(k, a, spot).wait_recv()
        return (
            f32(held[k], (p, q, spot))
            + f32(crossed[k], (p, q, spot))
            + f32(first_in[k], (a, spot))
        )

    def stage_two(k):
        def one(spot, _):
            held[k][1, 0, spot] = gathered_sum(k, 1, 0, spot).astype(jnp.bfloat16)
            second_out(k, spot).start()
            return 0

        lax.fori_loop(0, lines, one, 0)

    def line_out(k, a, spot, way):
        boxes, send, recv, device = (
            (from_left, right_send, left_recv, right)
            if way == "right"
            else (from_right, left_send, right_recv, left)
        )
        source = held[k].at[0, a, spot]
        box = boxes[k].at[spot] if z_first[k] else boxes[k].at[a, spot]
        return remote(source, box, send.at[k, a, spot], recv.at[k, a, spot], device)

    def line_total(k, a, spot):
        total = gathered_sum(k, 0, a, spot)
        if z_first[k]:
            second_out(k, spot).wait_recv()
            total = total + f32(second_in[k], (spot,))
        return total

    def box_at(k, a, spot):
        return (spot,) if z_first[k] else (a, spot)

    def stage_line(k, a):
        def pass_on(spot, way):
            passing = (z < spot) if way == "right" else (z > spot)
            inner = (z > 0) if way == "right" else (z < last)

            @pl.when(passing)
            def _():
                held[k][0, a, spot] = line_total(k, a, spot).astype(jnp.bfloat16)

                @pl.when(inner)
                def _():
                    line_out(k, a, spot, way).wait_recv()
                    box = from_left if way == "right" else from_right
                    held[k][0, a, spot] = (
                        f32(held[k], (0, a, spot)) + f32(box[k], box_at(k, a, spot))
                    ).astype(jnp.bfloat16)

                line_out(k, a, spot, way).start()

        def one(step, _):
            pass_on(last - step, "right")
            pass_on(step, "left")
            return 0

        lax.fori_loop(0, lines, one, 0)

    def line_end(k, a):
        outs[k][...] = line_total(k, a, z)

        @pl.when(z > 0)
        def _():
            line_out(k, a, z, "right").wait_recv()
            outs[k][...] += f32(from_left[k], box_at(k, a, z))

        @pl.when(z < last)
        def _():
            line_out(k, a, z, "left").wait_recv()
            outs[k][...] += f32(from_right[k], box_at(k, a, z))

    b = KINDS.index("blocks")
    rest = [k for k in sequence if k != b]

    def last_out(k):
        return remote(
            held[k].at[0, 1, z],
            second_in[k].at[0],
            second_send.at[k, 0],
            second_recv.at[k, 0],
            q_mate,
        )

    for k in rest:
        stage_two(k)
    stage_line(b, 1)
    stage_line(b, 0)
    for k in rest:
        stage_line(k, 0)
    line_end(b, 1)
    held[b][0, 1, z] = outs[b][...].astype(jnp.bfloat16)
    last_out(b).start()
    line_end(b, 0)
    last_out(b).wait_recv()
    outs[b][...] += f32(second_in[b], (0,))
    rows_low[...] = outs[b][...].astype(jnp.bfloat16)

    members, rows = shapes[b][0], shapes[b][1]
    my_rows = pl.ds(pl.multiple_of(place.dp * rows, rows), rows)
    owned = place.dp - place.core * members
    owner_here = (place.dp >= place.core * members) & (place.dp < (place.core + 1) * members)
    owner_there = (place.dp < 2 * members) & jnp.logical_not(owner_here)

    def row_copy(member):
        return remote(
            rows_low.at[member],
            whole_box.at[my_rows],
            row_send.at[member],
            row_recv.at[place.dp],
            (place.core * members + member, place.group),
        )

    def pair_copy(other):
        spot = pl.ds(pl.multiple_of(other * rows, rows), rows)
        return remote(
            whole_box.at[spot], whole_box.at[spot], pair_send.at[other], pair_recv.at[other], c_mate
        )

    for member in range(members):

        @pl.when(place.dp != place.core * members + member)
        def _(member=member):
            row_copy(member).start()

        @pl.when(place.dp == place.core * members + member)
        def _(member=member):
            whole_box[my_rows] = rows_low[member]
            pair_copy(place.dp).start()

    for k in rest:
        line_end(k, 0)
    square = jnp.sum(outs[b][...] * outs[b][...])
    for k in rest:
        square = square + jnp.sum(outs[k][...] * outs[k][...])
    square_out[...] = jnp.full(square_out.shape, square, jnp.float32)

    def dp_wait(other):
        dp_copy(other).wait_send()
        remote(dp_box.at[other], dp_box.at[other], dp_send.at[other], dp_recv.at[other], me).wait_recv()

    each_other(place.dp_size, place.dp, dp_wait)
    total = dp_box[0]
    for other in range(1, place.dp_size):
        total = total + dp_box[other]
    small_out[...] = total

    @pl.when(owner_here)
    def _():
        for other in range(place.dp_size):

            @pl.when(place.dp != other)
            def _(other=other):
                spot = pl.ds(other * rows, rows)
                remote(
                    rows_low.at[0], whole_box.at[spot], row_send.at[0], row_recv.at[other], me
                ).wait_recv()
                pair_copy(other).start()

        for other in range(place.dp_size):
            pair_copy(other).wait_send()

    @pl.when(owner_there)
    def _():
        for other in range(place.dp_size):
            pair_copy(other).wait_recv()

    @pl.when(place.dp < 2 * members)
    def _():
        whole_out[...] = whole_box[...]

    for member in range(members):

        @pl.when(place.dp != place.core * members + member)
        def _(member=member):
            row_copy(member).wait_send()

    last_out(b).wait_send()
    for k in range(count):

        def drain(spot, _, k=k):
            for p in range(2):
                for q in range(2):
                    cross_of(k, p, q, spot).wait_send()
            for a in range(2):
                first_out(k, a, spot).wait_send()
            if z_first[k]:
                second_out(k, spot).wait_send()
            for a in (0,) if z_first[k] else (0, 1):

                @pl.when(z < spot)
                def _():
                    line_out(k, a, spot, "right").wait_send()

                @pl.when(z > spot)
                def _():
                    line_out(k, a, spot, "left").wait_send()

            return 0

        lax.fori_loop(0, lines, drain, 0)


def reduce_gradients(sizes, pieces, shapes, small):
    dp_size, group_size = sizes
    lines, count = dp_size // 2, len(pieces)
    low = jnp.bfloat16

    def boxes(lead):
        return [
            pltpu.VMEM(tuple(lead(kind)) + tuple(shape), low) for kind, shape in zip(KINDS, shapes)
        ]

    dma = pltpu.SemaphoreType.DMA
    scratch = (
        boxes(lambda kind: (2, 2, lines))
        + boxes(lambda kind: (2, 2, lines))
        + boxes(lambda kind: (2, lines))
        + boxes(lambda kind: (1,) if kind == "blocks" else (lines,))
        + boxes(lambda kind: (2, lines) if kind == "blocks" else (lines,))
        + boxes(lambda kind: (2, lines) if kind == "blocks" else (lines,))
        + [
            pltpu.VMEM((group_size,) + small.shape, jnp.float32),
            pltpu.VMEM((dp_size,) + small.shape, jnp.float32),
            pltpu.VMEM(shapes[-1], low),
            pltpu.VMEM((D, D), low),
        ]
        + [dma((count, 2, 2, lines))] * 3
        + [dma((count, 2, lines))] * 2
        + [dma((count, lines))] * 2
        + [dma((count, 2, lines))] * 4
        + [dma((group_size,))] * 2
        + [dma((dp_size,))] * 2
        + [dma((shapes[-1][0],)), dma((dp_size,))]
        + [dma((dp_size,))] * 2
    )
    return pl.pallas_call(
        functools.partial(reduce_kernel, sizes, shapes),
        out_shape=[jax.ShapeDtypeStruct(shape, jnp.float32) for shape in shapes]
        + [
            jax.ShapeDtypeStruct(small.shape, jnp.float32),
            jax.ShapeDtypeStruct((8, 128), jnp.float32),
            jax.ShapeDtypeStruct((D, D), low),
        ],
        in_specs=[HBM] * count + [VMEM],
        out_specs=[VMEM] * (count + 3),
        scratch_shapes=scratch,
        name="reduce_gradients",
        compiler_params=pltpu.CompilerParams(
            collective_id=1, has_side_effects=True, vmem_limit_bytes=VMEM_LIMIT
        ),
    )(*pieces, small)


def shift_right(values, by):
    if by == 0:
        return values
    parts = []
    for first in range(0, values.shape[1], CLIP):
        part = values[:, first : first + CLIP]
        lane = lax.broadcasted_iota(jnp.int32, part.shape, 1)
        turned = pltpu.roll(part, by % CLIP, 1)
        inside = lane >= by if by > 0 else lane < CLIP + by
        parts.append(jnp.where(inside, turned, 0.0))
    return jnp.concatenate(parts, 1)


def place_windows(hidden, windows, taps):
    channels = hidden.shape[0]
    runs, half = taps // STRIDE, taps // STRIDE // 2
    for run in range(runs):
        by = STRIDE * (half - 1 - run) if run < half else -STRIDE * (run - half)
        windows[run * channels : (run + 1) * channels, :] = shift_right(hidden, by).astype(
            jnp.bfloat16
        )


def conv_group(hidden, weight_at, windows, taps, shape):
    channels = hidden.shape[0]
    chunks, _, _, chunk = shape
    place_windows(hidden, windows, taps)
    total = None
    for side in range(2):
        part = None
        for index in range(side * chunks // 2, (side + 1) * chunks // 2):
            term = dot(weight_at(index), windows[index * chunk : (index + 1) * chunk, :])
            part = term if part is None else part + term
        for offset in range(STRIDE):
            by = STRIDE - offset if side == 0 else -offset
            moved = shift_right(part[offset * channels : (offset + 1) * channels], by)
            total = moved if total is None else total + moved
    return total


def conv_group_back(hidden, grad, weight_at, put, windows, moved, taps, shape):
    channels = hidden.shape[0]
    chunks, _, _, chunk = shape
    half, runs = taps // STRIDE // 2, chunk // channels
    place_windows(hidden, windows, taps)
    total = None
    for side in range(2):
        for offset in range(STRIDE):
            by = offset - STRIDE if side == 0 else offset
            moved[offset * channels : (offset + 1) * channels, :] = shift_right(grad, by).astype(
                jnp.bfloat16
            )
        for index in range(side * chunks // 2, (side + 1) * chunks // 2):
            put(
                index,
                dot_nt(moved[...], windows[index * chunk : (index + 1) * chunk, :]).astype(
                    jnp.bfloat16
                ),
            )
            turned = dot_tn(weight_at(index), moved[...])
            for step in range(runs):
                run = index * runs + step
                by = -STRIDE * (half - 1 - run) if run < half else STRIDE * (run - half)
                part = shift_right(turned[step * channels : (step + 1) * channels], by)
                total = part if total is None else total + part
    return total


def over_rows(total, tile, action):
    def step(index, _):
        action(pl.ds(pl.multiple_of(index * tile, tile), tile))
        return 0

    lax.fori_loop(0, total // tile, step, 0)


def dot(one, two):
    return jnp.dot(one, two, preferred_element_type=jnp.float32)


def dot_nt(one, two):
    return lax.dot_general(one, two, (((1,), (1,)), ((), ())), preferred_element_type=jnp.float32)


def dot_tn(one, two):
    return lax.dot_general(one, two, (((0,), (0,)), ((), ())), preferred_element_type=jnp.float32)


def norm_parts(values):
    average = jnp.mean(values, -1, keepdims=True)
    centred = values - average
    inverse = lax.rsqrt(jnp.mean(centred * centred, -1, keepdims=True) + 1e-05)
    return centred * inverse, inverse


def norm_back(upstream, unit, inverse, gain):
    scaled = upstream * gain
    along = jnp.mean(scaled * unit, -1, keepdims=True)
    return inverse * (scaled - jnp.mean(scaled, -1, keepdims=True) - unit * along)


def gelu_pair(values):
    below = 0.5 + 0.5 * lax.erf(values * 0.7071067811865476)
    density = jnp.exp(values * values * -0.5) * 0.3989422804014327
    return values * below, below + values * density


def add_row(ref, row, values):
    ref[row : row + 1, :] += jnp.sum(values, 0, keepdims=True)


def front_kernel(taps, *refs):
    (
        features, mask, feature_norm, vectors, projection, kernel,
        feature_unit, normed, hidden_t, encoded, encoder_unit, encoder_inverse, slope,
        held, windows, hidden, out_t, load_sem,
    ) = refs
    frames = features.shape[0]
    groups = kernel.shape[1]
    channels = hidden_t.shape[0] // groups

    def load(group):
        return pltpu.make_async_copy(kernel.at[:, group], held.at[:, group], load_sem.at[group])

    for group in range(groups):
        load(group).start()

    def enter(at):
        unit, _ = norm_parts(features[at, :].astype(jnp.float32))
        feature_unit[at, :] = unit
        normed[at, :] = (unit * feature_norm[0:1, :] + feature_norm[1:2, :]).astype(jnp.bfloat16)

    over_rows(frames, 32, enter)
    projected = dot(normed[...], projection[...])
    hidden[...] = jnp.where(mask[...] > 0, vectors[0:1, :], projected)
    hidden_t[...] = hidden[...].T.astype(jnp.bfloat16)

    def one_group(group, _):
        load(group).wait()
        at = pl.ds(pl.multiple_of(group * channels, channels), channels)
        out_t[at, :] = conv_group(
            hidden_t[at, :].astype(jnp.float32), lambda index: held[index, group], windows, taps, kernel.shape
        )
        return 0

    lax.fori_loop(0, groups, one_group, 0)
    slope[...] = out_t[...].T

    def leave(at):
        active, derivative = gelu_pair(slope[at, :])
        slope[at, :] = derivative
        unit, inverse = norm_parts(hidden[at, :] + active)
        encoder_unit[at, :] = unit
        encoder_inverse[at, :] = inverse
        encoded[at, :] = unit * vectors[1:2, :] + vectors[2:3, :]

    over_rows(frames, 32, leave)


def front(features, mask, feature_norm, vectors, projection, kernel, taps):
    frames, width = features.shape
    chunks, groups, rows, chunk = kernel.shape
    full, low = jnp.float32, jnp.bfloat16
    out = jax.ShapeDtypeStruct
    return pl.pallas_call(
        functools.partial(front_kernel, taps),
        out_shape=[
            out((frames, width), full),
            out((frames, width), low),
            out((D, frames), low),
            out((frames, D), full),
            out((frames, D), full),
            out((frames, 1), full),
            out((frames, D), full),
        ],
        in_specs=[VMEM] * 5 + [HBM],
        out_specs=[VMEM] * 7,
        scratch_shapes=[
            pltpu.VMEM(kernel.shape, low),
            pltpu.VMEM((chunks * chunk, frames), low),
            pltpu.VMEM((frames, D), full),
            pltpu.VMEM((D, frames), full),
            pltpu.SemaphoreType.DMA((groups,)),
        ],
        name="front",
        compiler_params=pltpu.CompilerParams(vmem_limit_bytes=32 * 1024 * 1024),
    )(features, mask, feature_norm, vectors, projection, kernel)


def trunk_kernel(*refs):
    (
        encoded, mask, labels, scale, vectors, head, centers, blocks,
        encoded_grad, block_grad, head_grad, center_grad, rows_out,
        held, made, low, triple, attention, mixed, unit_one, inverse_one, middle, middle_low,
        active, slope, unit_two, inverse_two, work, work_low, flow_low, triple_grad, turned,
        load_sem, save_sem,
    ) = refs
    frames = encoded.shape[0]
    count = blocks.shape[0]
    ups = (count - 4) // 2
    tile = 32
    pairs = D // 128

    def load(block):
        return pltpu.make_async_copy(blocks.at[block], held.at[block], load_sem.at[block])

    def save(block):
        return pltpu.make_async_copy(made.at[block], block_grad.at[block], save_sem.at[block])

    for block in range(count):
        load(block).start()
    rows_out[...] = jnp.zeros_like(rows_out)

    def to_inputs(at):
        low[at, :] = encoded[at, :].astype(jnp.bfloat16)

    over_rows(frames, tile, to_inputs)

    def first_three(block, _):
        load(block).wait()
        triple[block] = dot(low[...], held[block]).astype(jnp.bfloat16)
        return 0

    lax.fori_loop(0, 3, first_three, 0)
    lane = lax.broadcasted_iota(jnp.int32, (CLIP, 128), 1)
    even = lane < HEAD

    def apart(values):
        zero = jnp.zeros_like(values)
        return jnp.concatenate([jnp.where(even, values, zero), jnp.where(even, zero, values)], 0)

    def beside(values):
        return jnp.concatenate([values[:CLIP], values[CLIP:]], 1)

    def spot(index):
        at = pl.ds(pl.multiple_of(index // pairs * CLIP, CLIP), CLIP)
        return at, pl.ds(pl.multiple_of(index % pairs * 128, 128), 128)

    def attend(index, _):
        at, lanes = spot(index)
        query, keys, values = triple[0, at, lanes], triple[1, at, lanes], triple[2, at, lanes]
        scores = dot_nt(apart(query), keys) * HEAD ** (-0.5)
        raised = jnp.exp(scores - jnp.max(scores, -1, keepdims=True))
        full = raised / jnp.sum(raised, -1, keepdims=True)
        attention[index] = full
        mixed[at, lanes] = dot(beside(full.astype(jnp.bfloat16)), apart(values)).astype(jnp.bfloat16)
        return 0

    lax.fori_loop(0, frames // CLIP * pairs, attend, 0)
    load(3).wait()
    work[...] = dot(mixed[...], held[3])

    def first_norm(at):
        unit, inverse = norm_parts(encoded[at, :] + work[at, :])
        unit_one[at, :] = unit
        inverse_one[at, :] = inverse
        value = unit * vectors[3:4, :] + vectors[4:5, :]
        middle[at, :] = value
        middle_low[at, :] = value.astype(jnp.bfloat16)

    over_rows(frames, tile, first_norm)

    def expand(step, _):
        load(4 + step).wait()
        slope[step] = dot(middle_low[...], held[4 + step])

        def bend(at):
            value, derivative = gelu_pair(slope[step, at, :])
            active[step, at, :] = value.astype(jnp.bfloat16)
            slope[step, at, :] = derivative

        over_rows(frames, tile, bend)
        return 0

    lax.fori_loop(0, ups, expand, 0)

    def contract(step, _):
        load(4 + ups + step).wait()
        middle[...] += dot(active[step], held[4 + ups + step])
        return 0

    lax.fori_loop(0, ups, contract, 0)

    def second_norm(at):
        unit, inverse = norm_parts(middle[at, :])
        unit_two[at, :] = unit
        inverse_two[at, :] = inverse
        flow_low[at, :] = (unit * vectors[5:6, :] + vectors[6:7, :]).astype(jnp.bfloat16)

    over_rows(frames, tile, second_norm)
    embedded = dot(flow_low[...], head[...])
    length = lax.rsqrt(jnp.sum(embedded * embedded, -1, keepdims=True) + 1e-06)
    unit_low = (embedded * length).astype(jnp.bfloat16)
    logits = dot_nt(unit_low, centers[...]) * inv_temp
    top = jnp.max(logits, -1, keepdims=True)
    raised = jnp.exp(logits - top)
    amount = jnp.sum(raised, -1, keepdims=True)
    choose = labels[...] == lax.broadcasted_iota(jnp.int32, logits.shape, 1)
    target = jnp.sum(jnp.where(choose, logits, 0.0), -1, keepdims=True)
    losses = mask[...] * (jnp.log(amount) + top - target)
    rows_out[7:8, :] = jnp.broadcast_to(jnp.sum(losses, 0, keepdims=True), (1, D))
    logit_grad = (
        (raised / amount - choose.astype(jnp.float32)) * (mask[...] * scale[0:1, 0:1])
    ).astype(jnp.bfloat16)
    unit_grad = dot(logit_grad, centers[...]) * inv_temp
    center_grad[...] = dot_tn(logit_grad, unit_low) * inv_temp
    along = jnp.sum(unit_grad * embedded, -1, keepdims=True)
    embedded_grad = (
        length * unit_grad - embedded * (length * length * length * along)
    ).astype(jnp.bfloat16)
    work[...] = dot_nt(embedded_grad, head[...])
    head_grad[...] = dot_tn(flow_low[...], embedded_grad).astype(jnp.bfloat16)

    def second_back(at):
        upstream = work[at, :]
        add_row(rows_out, 5, upstream * unit_two[at, :])
        add_row(rows_out, 6, upstream)
        value = norm_back(upstream, unit_two[at, :], inverse_two[at, :], vectors[5:6, :])
        middle[at, :] = value
        flow_low[at, :] = value.astype(jnp.bfloat16)

    over_rows(frames, tile, second_back)
    turned[...] = middle_low[...].T

    def feed_back(step, _):
        work[...] = dot_nt(flow_low[...], held[4 + ups + step])
        made[4 + ups + step] = dot_tn(active[step], flow_low[...]).astype(jnp.bfloat16)
        save(4 + ups + step).start()

        def bend(at):
            work_low[at, :] = (work[at, :] * slope[step, at, :]).astype(jnp.bfloat16)

        over_rows(frames, tile, bend)
        made[4 + step] = dot(turned[...], work_low[...]).astype(jnp.bfloat16)
        save(4 + step).start()
        middle[...] += dot_nt(work_low[...], held[4 + step])
        return 0

    lax.fori_loop(0, ups, feed_back, 0)

    def first_back(at):
        upstream = middle[at, :]
        add_row(rows_out, 3, upstream * unit_one[at, :])
        add_row(rows_out, 4, upstream)
        value = norm_back(upstream, unit_one[at, :], inverse_one[at, :], vectors[3:4, :])
        middle[at, :] = value
        flow_low[at, :] = value.astype(jnp.bfloat16)

    over_rows(frames, tile, first_back)
    made[3] = dot_tn(mixed[...], flow_low[...]).astype(jnp.bfloat16)
    save(3).start()
    work_low[...] = dot_nt(flow_low[...], held[3]).astype(jnp.bfloat16)

    def attend_back(index, _):
        at, lanes = spot(index)
        query, keys, values = triple[0, at, lanes], triple[1, at, lanes], triple[2, at, lanes]
        upstream = apart(work_low[at, lanes])
        full = attention[index]
        full_grad = dot_nt(upstream, values)
        triple_grad[2, at, lanes] = dot_tn(full.astype(jnp.bfloat16), upstream).astype(jnp.bfloat16)
        along = jnp.sum(full * full_grad, -1, keepdims=True)
        score_grad = (full * (full_grad - along)).astype(jnp.bfloat16)
        triple_grad[0, at, lanes] = (
            dot(beside(score_grad), apart(keys)) * HEAD ** (-0.5)
        ).astype(jnp.bfloat16)
        triple_grad[1, at, lanes] = (
            dot_tn(score_grad, apart(query)) * HEAD ** (-0.5)
        ).astype(jnp.bfloat16)
        return 0

    lax.fori_loop(0, frames // CLIP * pairs, attend_back, 0)
    turned[...] = low[...].T

    def last_three(block, _):
        made[block] = dot(turned[...], triple_grad[block]).astype(jnp.bfloat16)
        save(block).start()
        middle[...] += dot_nt(triple_grad[block], held[block])
        return 0

    lax.fori_loop(0, 3, last_three, 0)
    encoded_grad[...] = middle[...]
    for block in range(count):
        save(block).wait()


def trunk(encoded, mask, labels, scale, vectors, head, centers, blocks):
    frames, count = encoded.shape[0], blocks.shape[0]
    ups = (count - 4) // 2
    full, low = jnp.float32, jnp.bfloat16
    out = jax.ShapeDtypeStruct
    wide, wide_low = pltpu.VMEM((frames, D), full), pltpu.VMEM((frames, D), low)
    column = pltpu.VMEM((frames, 1), full)
    return pl.pallas_call(
        trunk_kernel,
        out_shape=[
            out((frames, D), full),
            out(blocks.shape, low),
            out(head.shape, low),
            out(centers.shape, full),
            out((8, D), full),
        ],
        in_specs=[VMEM] * 7 + [HBM],
        out_specs=[VMEM, HBM, VMEM, VMEM, VMEM],
        scratch_shapes=[
            pltpu.VMEM(blocks.shape, low),
            pltpu.VMEM(blocks.shape, low),
            wide_low,
            pltpu.VMEM((3, frames, D), low),
            pltpu.VMEM((frames // CLIP * D // 128, 2 * CLIP, CLIP), full),
            wide_low,
            wide,
            column,
            wide,
            wide_low,
            pltpu.VMEM((ups, frames, D), low),
            pltpu.VMEM((ups, frames, D), full),
            wide,
            column,
            wide,
            wide_low,
            wide_low,
            pltpu.VMEM((3, frames, D), low),
            pltpu.VMEM((D, frames), low),
            pltpu.SemaphoreType.DMA((count,)),
            pltpu.SemaphoreType.DMA((count,)),
        ],
        name="trunk",
        compiler_params=pltpu.CompilerParams(vmem_limit_bytes=VMEM_LIMIT),
    )(encoded, mask, labels, scale, vectors, head, centers, blocks)


def back_kernel(taps, *refs):
    (
        encoded_grad, mask, feature_norm, vectors, projection, feature_unit, normed, hidden_t,
        encoder_unit, encoder_inverse, slope, trunk_rows, kernel,
        kernel_grad, projection_grad, rows_out,
        held, made, windows, moved, grad, grad_t, through, through_t, load_sem, save_sem,
    ) = refs
    frames, width = feature_unit.shape
    groups = kernel.shape[1]
    channels = hidden_t.shape[0] // groups

    def load(group):
        return pltpu.make_async_copy(kernel.at[:, group], held.at[:, group], load_sem.at[group])

    def save(group):
        return pltpu.make_async_copy(made.at[:, group], kernel_grad.at[:, group], save_sem.at[group])

    for group in range(groups):
        load(group).start()
    rows_out[...] = jnp.zeros_like(rows_out)
    rows_out[0:8, :] = trunk_rows[...]

    def enter(at):
        upstream = encoded_grad[at, :]
        add_row(rows_out, 1, upstream * encoder_unit[at, :])
        add_row(rows_out, 2, upstream)
        value = norm_back(upstream, encoder_unit[at, :], encoder_inverse[at, :], vectors[1:2, :])
        grad[at, :] = value
        through[at, :] = value * slope[at, :]

    over_rows(frames, 32, enter)
    grad_t[...] = through[...].T.astype(jnp.bfloat16)

    def one_group(group, _):
        load(group).wait()
        at = pl.ds(pl.multiple_of(group * channels, channels), channels)

        def put(index, value):
            made[index, group] = value

        through_t[at, :] = conv_group_back(
            hidden_t[at, :].astype(jnp.float32),
            grad_t[at, :].astype(jnp.float32),
            lambda index: held[index, group],
            put,
            windows,
            moved,
            taps,
            kernel.shape,
        )
        save(group).start()
        return 0

    lax.fori_loop(0, groups, one_group, 0)
    through[...] = through_t[...].T

    def leave(at):
        total = grad[at, :] + through[at, :]
        inside = mask[at, :] > 0
        add_row(rows_out, 0, jnp.where(inside, total, 0.0))
        grad[at, :] = jnp.where(inside, 0.0, total)

    over_rows(frames, 32, leave)
    projected_grad = grad[...].astype(jnp.bfloat16)
    projection_grad[...] = dot_tn(normed[...], projected_grad).astype(jnp.bfloat16)
    normed_grad = dot_nt(projected_grad, projection[...])
    rows_out[8:9, 0:width] = jnp.sum(normed_grad * feature_unit[...], 0, keepdims=True)
    rows_out[9:10, 0:width] = jnp.sum(normed_grad, 0, keepdims=True)
    for group in range(groups):
        save(group).wait()


def back(encoded_grad, mask, feature_norm, vectors, projection, saved, trunk_rows, kernel, taps):
    chunks, groups, rows, chunk = kernel.shape
    feature_unit, normed, hidden_t, encoder_unit, encoder_inverse, slope = saved
    frames = encoded_grad.shape[0]
    full, low = jnp.float32, jnp.bfloat16
    out = jax.ShapeDtypeStruct
    return pl.pallas_call(
        functools.partial(back_kernel, taps),
        out_shape=[
            out(kernel.shape, low),
            out(projection.shape, low),
            out((16, D), full),
        ],
        in_specs=[VMEM] * 12 + [HBM],
        out_specs=[HBM, VMEM, VMEM],
        scratch_shapes=[
            pltpu.VMEM(kernel.shape, low),
            pltpu.VMEM(kernel.shape, low),
            pltpu.VMEM((chunks * chunk, frames), low),
            pltpu.VMEM((rows, frames), low),
            pltpu.VMEM((frames, D), full),
            pltpu.VMEM((D, frames), low),
            pltpu.VMEM((frames, D), full),
            pltpu.VMEM((D, frames), full),
            pltpu.SemaphoreType.DMA((groups,)),
            pltpu.SemaphoreType.DMA((groups,)),
        ],
        name="back",
        compiler_params=pltpu.CompilerParams(vmem_limit_bytes=48 * 1024 * 1024),
    )(
        encoded_grad, mask, feature_norm, vectors, projection, feature_unit, normed, hidden_t,
        encoder_unit, encoder_inverse, slope, trunk_rows, kernel,
    )


def local_step(weights, features, masks, labels, inverse_count):
    feature_norm, projection, vectors, kernel, head, centers_low, blocks = weights
    frames = features.shape[0] * features.shape[1] * CLIP
    taps = kernel.shape[0] * kernel.shape[3] // (D // kernel.shape[1]) * STRIDE
    mask = masks.reshape(frames, 1)
    feature_unit, normed, hidden_t, encoded, encoder_unit, encoder_inverse, slope = front(
        features.reshape(frames, -1), mask, feature_norm, vectors, projection, kernel, taps
    )
    encoded_grad, block_grad, head_grad, center_grad, trunk_rows = trunk(
        encoded,
        mask,
        labels.reshape(frames, 1),
        jnp.full((8, 128), inverse_count),
        vectors,
        head,
        centers_low,
        blocks,
    )
    kernel_grad, projection_grad, rows = back(
        encoded_grad,
        mask,
        feature_norm,
        vectors,
        projection,
        (feature_unit, normed, hidden_t, encoder_unit, encoder_inverse, slope),
        trunk_rows,
        kernel,
        taps,
    )
    return rows, projection_grad, kernel_grad, head_grad, center_grad, block_grad


def roots_kernel(sizes, members, *refs):
    (
        whole, stat, square_in, extra_in, sides_out, update_out, square_out,
        big, low, m0, m0b, m1, m1b, s1, s1b, s2b, s3, s3b, root, mixed,
        group_box, dp_box, group_send, group_recv, dp_send, dp_recv,
        side_send, side_recv, side_own, mixed_send, mixed_recv, update_send, update_recv, update_own,
    ) = refs
    place = Place(*sizes)
    dp_size, rows = place.dp_size, D // place.dp_size
    me, c_mate = (place.dp, place.group), place.at(place.z, 0, 0, 1)
    owner = place.dp < 2 * members
    owned_group = place.x * 2 + place.dp // members
    owned_member = place.dp % members
    tile = 256
    greet(place)

    def remote(source, target, send, recv, device):
        return pltpu.make_async_remote_copy(
            src_ref=source,
            dst_ref=target,
            send_sem=send,
            recv_sem=recv,
            device_id=device,
            device_id_type=MESH,
        )

    def each_other(size, mine, action):
        for other in range(size):
            pl.when(mine != other)(functools.partial(action, other))

    def group_copy(other, slot):
        return remote(
            group_box.at[slot], group_box.at[slot], group_send.at[other], group_recv.at[slot], (place.dp, other)
        )

    def dp_copy(other, slot):
        return remote(dp_box.at[slot], dp_box.at[slot], dp_send.at[other], dp_recv.at[slot], (other, place.group))

    group_box[place.group] = square_in[...]
    each_other(place.group_size, place.group, lambda other: group_copy(other, place.group).start())

    def product_rows(one, two, then):
        def step(index, _):
            at = pl.ds(pl.multiple_of(index * tile, tile), tile)
            then(at, jnp.dot(one[at, :], two[...], preferred_element_type=jnp.float32))
            return 0

        lax.fori_loop(0, D // tile, step, 0)

    def side_copy(other):
        spot = pl.ds(pl.multiple_of(other * rows, rows), rows)
        return remote(
            low.at[spot],
            sides_out.at[owned_member, place.core],
            side_send.at[other],
            side_recv.at[owned_member, place.core],
            (other, owned_group),
        )

    def side_local():
        spot = pl.ds(pl.multiple_of(place.dp * rows, rows), rows)
        return pltpu.make_async_copy(low.at[spot], sides_out.at[owned_member, place.core], side_own)

    mine = place.group == owned_group

    def to_rows(other, remote_action, local_action):
        away = (place.dp != other) | jnp.logical_not(mine)
        pl.when(away)(functools.partial(remote_action, other))
        pl.when(jnp.logical_not(away))(local_action)

    @pl.when(owner)
    def _():
        @pl.when(place.core == 0)
        def _():
            def step(index, _):
                at = pl.ds(pl.multiple_of(index * tile, tile), tile)
                value = lax.dot_general(
                    whole[at, :],
                    whole[...],
                    (((1,), (1,)), ((), ())),
                    preferred_element_type=jnp.float32,
                )
                big[at, :] = value
                low[at, :] = value.astype(jnp.bfloat16)
                return 0

            lax.fori_loop(0, D // tile, step, 0)

        @pl.when(place.core == 1)
        def _():
            s1b[...] = whole[...].T

            def keep(at, value):
                big[at, :] = value
                low[at, :] = value.astype(jnp.bfloat16)

            product_rows(s1b, whole, keep)

        for other in range(dp_size):
            to_rows(other, lambda other: side_copy(other).start(), lambda: side_local().start())

    def group_wait(other):
        group_copy(other, place.group).wait_send()
        group_copy(other, other).wait_recv()

    each_other(place.group_size, place.group, group_wait)
    total = group_box[0]
    for other in range(1, place.group_size):
        total = total + group_box[other]
    dp_box[place.dp] = total
    each_other(dp_size, place.dp, lambda other: dp_copy(other, place.dp).start())

    def dp_wait(other):
        dp_copy(other, place.dp).wait_send()
        dp_copy(other, other).wait_recv()

    each_other(dp_size, place.dp, dp_wait)
    total = dp_box[0]
    for other in range(1, dp_size):
        total = total + dp_box[other]
    total = total + extra_in[...]
    square_out[...] = total

    @pl.when(owner)
    def _():
        factor = jnp.minimum(1.0, max_norm / (jnp.sqrt(total[0:1, 0:1]) + 1e-06))
        square_factor = factor * factor
        spread_f = (1 - stat_decay) * square_factor

        def diagonal(at_start, shape):
            row = lax.broadcasted_iota(jnp.int32, shape, 0) + at_start
            return row == lax.broadcasted_iota(jnp.int32, shape, 1)

        def each_tile(action, carry):
            def step(index, carry):
                start = pl.multiple_of(index * tile, tile)
                return action(pl.ds(start, tile), start, carry)

            return lax.fori_loop(0, D // tile, step, carry)

        def renew(at, start, trace):
            value = stat_decay * stat[at, :].astype(jnp.float32) + spread_f * big[at, :]
            big[at, :] = value
            on = jnp.where(diagonal(start, value.shape), value, 0.0)
            return trace + jnp.sum(jnp.sum(on, 1, keepdims=True), 0, keepdims=True)

        trace = each_tile(renew, jnp.zeros((1, 1), jnp.float32))
        damping = 0.0001 * (trace / D)

        def damp(at, start, total):
            value = big[at, :]
            value = value + jnp.where(diagonal(start, value.shape), damping, 0.0)
            big[at, :] = value
            return total + jnp.sum(jnp.sum(value * value, 1, keepdims=True), 0, keepdims=True)

        magnitude = jnp.sqrt(each_tile(damp, jnp.zeros((1, 1), jnp.float32)))

        def scale(at, start, carry):
            value = big[at, :] / magnitude
            m0[at, :] = value
            m0b[at, :] = value.astype(jnp.bfloat16)
            return carry

        each_tile(scale, 0)
        a = 1.5625

        def square_of(source):
            def then(at, value):
                value = value * 0.0625 - 0.625 * source[at, :]
                s1[at, :] = value
                s1b[at, :] = value.astype(jnp.bfloat16)

            return then

        def fourth(at, value):
            s2b[at, :] = (value + (2 * a) * s1[at, :]).astype(jnp.bfloat16)

        product_rows(m0b, m0b, square_of(m0))
        product_rows(s1b, s1b, fourth)

        def next_one(at, value):
            value = value + (a * a) * m0[at, :]
            m1[at, :] = value
            m1b[at, :] = value.astype(jnp.bfloat16)

        product_rows(s2b, m0b, next_one)

        def joined(at, value):
            value = value * 0.0625 - 0.3125 * (m0[at, :] + m1[at, :])
            s3[at, :] = value
            s3b[at, :] = value.astype(jnp.bfloat16)

        product_rows(m0b, m1b, joined)
        product_rows(m1b, m1b, square_of(m1))
        product_rows(s1b, s1b, fourth)

        def next_two(at, value):
            value = value + (a * a) * m1[at, :]
            m0[at, :] = value
            m0b[at, :] = value.astype(jnp.bfloat16)

        product_rows(s2b, m1b, next_two)
        outer = lax.rsqrt(jnp.sqrt(magnitude))

        def final(at, value):
            value = 1.25 * s3[at, :] - (0.25 * a) * m0[at, :] - 0.25 * value
            start = at.start
            value = value + jnp.where(diagonal(start, value.shape), 1.25 * a, 0.0)
            root[at, :] = (value * outer).astype(jnp.bfloat16)

        product_rows(s3b, m0b, final)

    def mixed_copy():
        return remote(mixed, mixed, mixed_send, mixed_recv, c_mate)

    def update_copy(other):
        spot = pl.ds(pl.multiple_of(other * rows, rows), rows)
        return remote(
            m1b.at[spot],
            update_out.at[owned_member],
            update_send.at[other],
            update_recv.at[owned_member],
            (other, owned_group),
        )

    def update_local():
        spot = pl.ds(pl.multiple_of(place.dp * rows, rows), rows)
        return pltpu.make_async_copy(m1b.at[spot], update_out.at[owned_member], update_own)

    @pl.when(owner & (place.core == 0))
    def _():
        def keep(at, value):
            mixed[at, :] = value.astype(jnp.bfloat16)

        product_rows(root, whole, keep)
        mixed_copy().start()
        mixed_copy().wait_send()

    @pl.when(owner & (place.core == 1))
    def _():
        mixed_copy().wait_recv()

        def keep(at, value):
            m1b[at, :] = value.astype(jnp.bfloat16)

        product_rows(mixed, root, keep)
        for other in range(dp_size):
            to_rows(other, lambda other: update_copy(other).start(), lambda: update_local().start())
        for other in range(dp_size):
            to_rows(other, lambda other: update_copy(other).wait_send(), lambda: update_local().wait())

    @pl.when(owner)
    def _():
        for other in range(dp_size):
            to_rows(other, lambda other: side_copy(other).wait_send(), lambda: side_local().wait())

    for member in range(members):
        holder = place.core * members + member
        for side in range(2):

            @pl.when((place.dp != holder) | (place.core != side))
            def _(member=member, side=side):
                remote(
                    low.at[pl.ds(0, rows)],
                    sides_out.at[member, side],
                    side_send.at[0],
                    side_recv.at[member, side],
                    me,
                ).wait_recv()

        @pl.when((place.dp != holder) | (place.core != 1))
        def _(member=member):
            remote(
                m1b.at[pl.ds(0, rows)],
                update_out.at[member],
                update_send.at[0],
                update_recv.at[member],
                me,
            ).wait_recv()


def shampoo_roots(sizes, members, whole, stat, square, extra):
    dp_size, group_size = sizes
    rows = D // dp_size
    low, full = jnp.bfloat16, jnp.float32
    dma = pltpu.SemaphoreType.DMA
    half, word = pltpu.VMEM((D, D), low), pltpu.VMEM((D, D), full)
    return pl.pallas_call(
        functools.partial(roots_kernel, sizes, members),
        out_shape=[
            jax.ShapeDtypeStruct((members, 2, rows, D), low),
            jax.ShapeDtypeStruct((members, rows, D), low),
            jax.ShapeDtypeStruct((8, 128), full),
        ],
        in_specs=[VMEM] * 4,
        out_specs=[VMEM] * 3,
        scratch_shapes=[word, half, word, half, word, half, word, half, half, word, half, half, half]
        + [pltpu.VMEM((group_size, 8, 128), full), pltpu.VMEM((dp_size, 8, 128), full)]
        + [dma((group_size,))] * 2
        + [dma((dp_size,))] * 2
        + [dma((dp_size,)), dma((members, 2)), dma]
        + [dma, dma]
        + [dma((dp_size,)), dma((members,)), dma],
        name="shampoo_roots",
        compiler_params=pltpu.CompilerParams(
            collective_id=2, has_side_effects=True, vmem_limit_bytes=VMEM_LIMIT
        ),
    )(whole, stat, square, extra)


def conv_to_shard(weight):
    taps, c, channels = weight.shape
    split = weight.reshape(taps // STRIDE, STRIDE, c, channels // c, c)
    return split.transpose(3, 1, 4, 0, 2).reshape(channels // c, STRIDE * c, taps // STRIDE * c)


def conv_from_shard(shard):
    groups, rows, columns = shard.shape
    c = rows // STRIDE
    split = shard.reshape(groups, STRIDE, c, columns // c, c)
    return split.transpose(3, 1, 4, 0, 2).reshape(columns // c * STRIDE, c, groups * c)


def pack_small(projection, head, clusters, note):
    lead, kind = projection.shape[:-2], projection.dtype
    spare = jnp.broadcast_to(note, lead + (96, 64)).astype(kind)
    padded = jnp.concatenate([clusters, jnp.zeros(lead + (2, 32), kind)], -2)
    return jnp.concatenate(
        [
            projection[..., :128],
            jnp.concatenate([projection[..., 128:], jnp.zeros(lead + (64, 64), kind)], -1),
            jnp.concatenate([head, spare], -1),
            jnp.concatenate([padded[..., 32 * j : 32 * j + 32, :] for j in range(4)], -1),
        ],
        -2,
    )


def unpack_small(packed):
    projection = jnp.concatenate([packed[..., :64, :], packed[..., 64:128, :64]], -1)
    head = packed[..., 128:224, :64]
    clusters = jnp.concatenate(
        [packed[..., 224:, 32 * j : 32 * j + 32] for j in range(4)], -2
    )[..., :126, :]
    return projection, head, clusters, packed[..., 128, 64]


def parts_of_rows(rows, vector_rows, width):
    return rows[:vector_rows], rows[vector_rows + 1 : vector_rows + 3, :width], rows[vector_rows, 0]


SMALL = ((64, 192), (96, 64), (126, 32))


def body(
    sizes,
    features,
    span_starts,
    labels,
    feature_norm,
    feature_first,
    feature_second,
    projection,
    projection_first,
    projection_second,
    vectors,
    vector_first,
    vector_second,
    conv_weight,
    conv_first,
    conv_second,
    head,
    head_first,
    head_second,
    clusters,
    cluster_first,
    cluster_second,
    blocks,
    statistics,
):
    dp_size, group_size = sizes
    members, rows = blocks.shape[0], blocks.shape[1]
    fast = (
        rows % 16 == 0
        and dp_size % 2 == 0
        and group_size == 4
        and dp_size >= 2 * members
        and (projection.shape, head.shape, clusters.shape) == SMALL
        and conv_weight.shape[2] % conv_weight.shape[1] == 0
    )
    masks = jax.vmap(jax.vmap(frame_mask))(span_starts)
    local_count = jnp.sum(masks)
    if fast:
        pieces = (
            conv_to_shard(to_low(conv_weight)),
            pack_small(to_low(projection), to_low(head), to_low(clusters), to_low(local_count)),
            to_low(blocks),
        )
        shapes = [piece.shape for piece in pieces]
        kernel_w, small_w, blocks_w, stat_whole = gather_weights(sizes, pieces, to_low(statistics))
        proj_s, head_s, clusters_s, counts = unpack_small(small_w)
        proj_w = proj_s.transpose(0, 2, 1, 3).reshape(dp_size * SMALL[0][0], -1)
        head_w = head_s.transpose(0, 2, 1, 3).reshape(dp_size * SMALL[1][0], -1)
        clusters_w = clusters_s.transpose(1, 2, 0, 3).reshape(group_size * SMALL[2][0], -1)
        masked_count = jnp.sum(counts.astype(jnp.float32))
    else:
        proj_w, kernel_full, head_w, clusters_w, blocks_w = gather_plain(
            projection, conv_weight, head, clusters, blocks
        )
        whole = conv_to_shard(kernel_full)
        kernel_w = whole.reshape(whole.shape[:2] + (4, -1)).transpose(2, 0, 1, 3)
        masked_count = lax.psum(local_count, ("dp", "group"))
    center_table = clusters_w.astype(jnp.float32)
    _, center_back = jax.vjp(unit_rows, center_table)
    weights = (
        feature_norm,
        proj_w,
        vectors,
        kernel_w,
        head_w,
        to_low(unit_rows(center_table)),
        blocks_w,
    )
    row_part, proj_part, kernel_part, head_part, center_part, block_part = local_step(
        weights, features, masks, labels, 1.0 / masked_count
    )
    vector_rows, width = vectors.shape[0], feature_norm.shape[1]
    center_part = center_back(center_part)[0]
    if fast:
        small_part = pack_small(
            proj_part.reshape(dp_size, SMALL[0][0], group_size, -1).transpose(0, 2, 1, 3),
            head_part.reshape(dp_size, SMALL[1][0], group_size, -1).transpose(0, 2, 1, 3),
            to_low(center_part).reshape(group_size, SMALL[2][0], dp_size, -1).transpose(2, 0, 1, 3),
            jnp.zeros((), jnp.bfloat16),
        )
        kernel_sum, small_sum, block_sum, extra, square, whole = reduce_gradients(
            sizes, (kernel_part, small_part, block_part), shapes, row_part
        )
        vector_grad, feature_grad, loss_sum = parts_of_rows(extra, vector_rows, width)
        proj_sum, head_sum, cluster_sum, _ = unpack_small(small_sum)
        large_total = (proj_sum, conv_from_shard(kernel_sum), head_sum, cluster_sum, block_sum)
        replicated = jnp.sum(feature_grad * feature_grad) + jnp.sum(vector_grad * vector_grad)
        sides, update_rows, square = shampoo_roots(
            sizes, members, whole, stat_whole, square, jnp.full((8, 128), replicated)
        )
        norm_square = square[0, 0]
    else:
        kernel_plain = conv_from_shard(
            kernel_part.transpose(1, 2, 0, 3).reshape(kernel_part.shape[1:3] + (-1,))
        )
        large_total = reduce_grads(
            tuple(
                part.astype(jnp.float32)
                for part in (proj_part, kernel_plain, head_part, center_part, block_part)
            )
        )
        vector_grad, feature_grad, loss_sum = parts_of_rows(
            lax.psum(row_part, ("dp", "group")), vector_rows, width
        )
        local_squares = sum((jnp.sum(part * part) for part in large_total))
        norm_square = (
            lax.psum(local_squares, ("dp", "group"))
            + jnp.sum(feature_grad * feature_grad)
            + jnp.sum(vector_grad * vector_grad)
        )
    grad_norm = jnp.sqrt(norm_square)
    factor = jnp.minimum(1.0, max_norm / (grad_norm + 1e-06))
    proj_grad, kernel_grad, head_grad, cluster_grad, block_rows = [
        part * factor for part in large_total
    ]
    feature_out = adamw(
        feature_norm, feature_grad * factor, feature_first, feature_second, rate_vector, 0.0
    )
    projection_out = adamw(
        projection, proj_grad, projection_first, projection_second, rate_matrix, decay_weight
    )
    vector_out = adamw(vectors, vector_grad * factor, vector_first, vector_second, rate_vector, 0.0)
    conv_out = adamw(conv_weight, kernel_grad, conv_first, conv_second, rate_matrix, decay_weight)
    head_out = adamw(head, head_grad, head_first, head_second, rate_matrix, decay_weight)
    cluster_out = adamw(
        clusters, cluster_grad, cluster_first, cluster_second, rate_matrix, decay_weight
    )
    if fast:
        statistics_new = stat_decay * statistics + (1 - stat_decay) * factor * factor * sides.astype(
            jnp.float32
        )
        update_rows = update_rows.astype(jnp.float32) * factor
    else:
        statistics_new, update_rows = shampoo_plain(block_rows, statistics)
    blocks_new = blocks - rate_shampoo * (update_rows + decay_weight * blocks)
    return (
        loss_sum,
        masked_count,
        grad_norm,
        *feature_out,
        *projection_out,
        *vector_out,
        *conv_out,
        *head_out,
        *cluster_out,
        block_rows,
        statistics_new,
        blocks_new,
    )


def solution(mesh):
    in_specs = (
        P(None, ("dp", "group"), None, None),
        P(None, ("dp", "group"), None),
        P(None, ("dp", "group"), None),
        P(),
        P(),
        P(),
        P("dp", "group"),
        P("dp", "group"),
        P("dp", "group"),
        P(),
        P(),
        P(),
        P("group", None, "dp"),
        P("group", None, "dp"),
        P("group", None, "dp"),
        P("dp", "group"),
        P("dp", "group"),
        P("dp", "group"),
        P("group", "dp"),
        P("group", "dp"),
        P("group", "dp"),
        P("group", "dp", None),
        P("group", None, "dp", None),
    )
    out_specs = (
        P(),
        P(),
        P(),
        P(),
        P(),
        P(),
        P("dp", "group"),
        P("dp", "group"),
        P("dp", "group"),
        P(),
        P(),
        P(),
        P("group", None, "dp"),
        P("group", None, "dp"),
        P("group", None, "dp"),
        P("dp", "group"),
        P("dp", "group"),
        P("dp", "group"),
        P("group", "dp"),
        P("group", "dp"),
        P("group", "dp"),
        P("group", "dp", None),
        P("group", None, "dp", None),
        P("group", "dp", None),
    )
    return jax.shard_map(
        functools.partial(body, (mesh.shape["dp"], mesh.shape["group"])), mesh=mesh, in_specs=in_specs, out_specs=out_specs, check_vma=False)
```

time: 2500 us -> 518 us (0.21)
  waiting for transfers between devices: 1140 us -> 0 us
  local copies, waits for them, and re-layouts: 541 us -> 53.6 us
  Pallas kernels: 0 us -> 425 us
  matrix products: 248 us -> 0 us
  blocking collectives: 209 us -> 0 us
  loops' own time: 181 us -> 0 us
  other arithmetic: 129 us -> 26.4 us
    pallas_call x0 -> x6, Pallas kernels: none -> 425 us  [the longest x1 157 us: reduce_gradients(): pl.pallas_call(functools.partial(reduce_kernel, sizes, shapes), out_shape...]
    unnamed x22 -> x0, waiting for transfers between devices: 328 us -> none
    reduce_scatter x5 -> x0, waiting for transfers between devices: 305 us -> none  [the longest x1 177 us: reduce_grads(): lax.psum_scatter(block_part, 'group', scatter_dimension=0, tiled=True)]
    psum x1 -> x0, waiting for transfers between devices: 277 us -> none  [spread_2(): return lax.psum(jnp.where(mine, array, jnp.zeros_like(array)), axis)]
    dot_general x106 -> x0, matrix products: 248 us -> none  [the longest x102 234 us: product(): return jnp.einsum(spec, left, right, preferred_element_type=jnp.float32)]
    all_gather x7 -> x0, waiting for transfers between devices: 231 us -> none  [the longest x1 96.5 us: body(): lax.all_gather(to_low(conv_weight), 'dp', axis=2, tiled=True)]
    another operation x12 -> x0, loops' own time: 181 us -> none  [the longest x4 90.3 us: conv_apply(): lax.scan(one_block, jnp.zeros((frames, groups, group_width), jnp.float32)...]
    unnamed x447 -> x119, local copies, waits for them, and re-layouts: 142 us -> 23.5 us
  transfers between devices with their start and end apart: 18 -> 0, of which waited for: 12 -> 0; matrix products, arithmetic and copies ran while one was open for 34% -> 0% of each run, Pallas kernels for 0% -> 0%
where the time goes in v1:
time: 518 us; the launch traced here: 511 us
  Pallas kernels  425 us (82%)
  local copies, waits for them, and re-layouts  53.6 us (10%)
  other arithmetic  26.4 us (5%)
  between operations  5.81 us (1%)
    pallas_call x1, Pallas kernels, reduce_gradients(): pl.pallas_call(functools.partial(reduce_kernel, sizes, shapes), out_shape...  157 us
    pallas_call x1, Pallas kernels, gather_weights(): pl.pallas_call(functools.partial(gather_kernel, sizes, shapes), out_shape...  113 us
    pallas_call x1, Pallas kernels, shampoo_roots(): pl.pallas_call(functools.partial(roots_kernel, sizes, members), out_shape...  77.1 us
    pallas_call x1, Pallas kernels, trunk(): pl.pallas_call(trunk_kernel, out_shape=[out((frames, D), full), out(block...  41.1 us
    unnamed x119, local copies, waits for them, and re-layouts  23.5 us
    pallas_call x1, Pallas kernels, back(): pl.pallas_call(functools.partial(back_kernel, taps), out_shape=[out(kerne...  22.1 us
    pallas_call x1, Pallas kernels, front(): pl.pallas_call(functools.partial(front_kernel, taps), out_shape=[out((fra...  14.7 us

profile of v1, /device:TPU:13, one launch (start us, length us, event | category | flops | bytes accessed | tf_op | source)
XLA Modules:
  0.0 510.6 jit_solution(3930036936606138429)
XLA Ops:
  0.7 0.8 copy.174
  1.5 0.7 broadcast_add_fusion.1
  2.2 0.8 fusion.23
  3.0 0.6 convert_reduce_fusion.1
  3.6 0.8 convert_element_type.73
  4.4 0.8 convert_element_type.74
  5.3 0.7 fusion.16.refs_1_
  6.0 1.2 convert_element_type.72
  7.6 1.9 copy.172
  9.5 1.9 reshape.158.refs_0_
  11.6 112.6 %gather_weights.1 = (bf16[4,16,192,384]{3,2,1,0:T(8,128)(2,1)S(1)}, bf16[8,4,256,128]{3,2,1,0:T(8,128)(2,1)S(1)}, bf16[12,768,768]{2,1,0:T(8,128)(2,1)S(1)}, bf16[768,768]{1,0:T(8,128)(2,1)S(1)}) custom-call(bf16[2,192,384]{2,1,0:T(8,128)(2,1)S(1)} %reshape.158.refs_0_, bf16[256,128]{1,0:T(8,128)(2,1)S(1)} %fusion.16.refs_1_, ...), custom_call_target="tpu_custom_call" | custom-call | tf_op jit(solution)/shard_map/gather_weights/pallas_call | solution.py:447
  124.2 3.7 copy-done
  127.8 5.0 copy-done.2
  132.9 1.0 copy-done.5
  134.9 0.4 fusion.8
  135.4 0.3 copy.182
  136.3 0.8 multiply_convert_fusion.refs_6_
  137.5 1.8 copy.175
  139.4 2.4 reshape.159.refs_4_
  142.0 3.7 copy-done.1
  145.7 14.7 %front.1 = (f32[256,512]{1,0:T(8,128)S(1)}, bf16[256,512]{1,0:T(8,128)(2,1)S(1)}, bf16[768,256]{1,0:T(8,128)(2,1)S(1)}, f32[256,768]{1,0:T(8,128)S(1)}, f32[256,...) custom-call(bf16[256,512]{1,0:T(8,128)(2,1)S(1)} %bitcast.27, f32[256,1]{1,0:T(8,128)S(1)} %copy.176.refs_1_, ...), custom_call_target="tpu_custom_call" | custom-call | tf_op jit(solution)/shard_map/front/pallas_call | solution.py:1030
  160.4 0.9 copy-done.6
  161.3 0.9 copy-done.7
  162.2 0.9 copy-done.9
  163.0 0.8 copy-done.13
  163.8 0.7 copy-done.15
  164.6 0.7 copy-done.20
  165.3 0.7 convert_reduce_fusion
  166.7 0.6 broadcast_in_dim.6.refs_3_
  167.3 0.4 copy.208
  167.7 1.2 reshape.167.refs_5_
  169.0 0.8 copy.185.refs_2_
  169.8 41.1 %trunk.1 = (f32[256,768]{1,0:T(8,128)}, bf16[12,768,768]{2,1,0:T(8,128)(2,1)}, bf16[768,256]{1,0:T(8,128)(2,1)}, f32[504,256]{1,0:T(8,128)}, f32[8,768]{1,0:T(8,128)}) custom-call(f32[256,768]{1,0:T(8,128)} %copy-done.6, f32[256,1]{1,0:T(8,128)} %copy-done.3, s32[256,1]{1,0:T(8,128)} %copy.185.refs_2_, f32[8,128]{1,0:T(8,128)} %broadcast_in_dim.6.refs_3_, ...), custom_call_target="tpu_custom_call" | custom-call | tf_op jit(solution)/shard_map/trunk/pallas_call | solution.py:1258
  210.9 1.2 multiply_reduce_fusion
  212.1 1.2 fusion.9
  213.5 0.9 reshape.164
  214.4 2.8 copy.194
  217.2 2.4 fusion.32
  219.7 22.1 %back.1 = (bf16[4,16,192,384]{3,2,1,0:T(8,128)(2,1)}, bf16[512,768]{1,0:T(8,128)(2,1)S(1)}, f32[16,768]{1,0:T(8,128)S(1)}) custom-call(f32[256,768]{1,0:T(8,128)S(1)} %copy-done.11, f32[256,1]{1,0:T(8,128)S(1)} %copy-done.4, f32[2,512]{1,0:T(2,128)S(1)} %copy-done.23, f32[7,768]{1,0:T(8,128)S(1)} %copy-done.18, bf16[512,768]{1,0:T(8,128)(2,1)S(1)} %reshape.159.refs_4_, ...), custom_call_target="tpu_custom_call" | custom-call | tf_op jit(solution)/shard_map/back/pallas_call | solution.py:1375
  241.8 0.9 copy-done.12
  242.7 0.6 copy-done.22
  243.3 2.7 reshape.162
  246.4 1.9 reshape.168
  248.5 2.9 fusion.5.refs_1_
  251.5 157.4 %reduce_gradients.1 = (f32[2,192,384]{2,1,0:T(8,128)}, f32[256,128]{1,0:T(8,128)}, f32[3,96,768]{2,1,0:T(8,128)}, f32[16,768]{1,0:T(8,128)}, f32[8,128]{1,0:T(8,128)}, /*index=5*/bf16[768,768]{1,0:T(8,128)(2,1)}) custom-call(bf16[4,16,192,384]{3,2,1,0:T(8,128)(2,1)} %get-tuple-element.64.refs_0_, bf16[8,4,256,128]{3,2,1,0:T(8,128)(2,1)} %fusion.5.refs_1_, ...), custom_call_target="tpu_custom_call" | custom-call | tf_op jit(solution)/shard_map/reduce_gradients/pallas_call | solution.py:848
  408.9 1.5 multiply_reduce_fusion.1
  410.3 1.3 multiply_reduce_fusion.2
  413.0 0.6 broadcast_in_dim.8.refs_3_
  413.6 77.1 %shampoo_roots.1 = (bf16[3,2,96,768]{3,2,1,0:T(8,128)(2,1)}, bf16[3,96,768]{2,1,0:T(8,128)(2,1)}, f32[8,128]{1,0:T(8,128)}) custom-call(bf16[768,768]{1,0:T(8,128)(2,1)} %get-tuple-element.71.refs_0_, bf16[768,768]{1,0:T(8,128)(2,1)} %copy-done.5, f32[8,128]{1,0:T(8,128)} %get-tuple-element.73.refs_2_, f32[8,128]{1,0:T(8,128)} %broadcast_in_dim.8.refs_3_), custom_call_target="tpu_custom_call" | custom-call | tf_op jit(solution)/shard_map/shampoo_roots/pallas_call | solution.py:1723
  490.6 1.2 slice.123
  492.6 2.8 multiply_add_fusion
  495.4 1.4 multiply_subtract_fusion
  497.3 0.7 multiply_subtract_fusion.5
  498.3 0.7 copy.205
  499.0 0.7 copy.206
  499.7 0.7 copy.207
  500.5 0.6 mul.398
  501.1 1.0 copy.195
  502.1 0.9 mul.400
  503.3 3.2 multiply_subtract_fusion.1
  506.5 0.6 multiply_subtract_fusion.4
  507.2 0.7 multiply_subtract_fusion.2
  507.9 0.6 multiply_subtract_fusion.6
  508.6 0.5 slice.120
  (142 shorter events, 4.6 us)
Async XLA Ops:
  7.2 4.2 copy-start.27
  9.5 2.0 copy-start.29
  124.2 3.7 copy-start
  127.8 5.0 copy-start.2
  132.9 1.0 copy-start.5
  136.2 1.3 copy-start.25
  137.5 4.4 copy-start.17
  137.5 4.4 copy-start.19
  137.5 4.4 copy-start.23
  141.9 18.5 %copy-start.3 = (f32[256,1]{1,0:T(8,128)}, f32[256,1]{1,0:T(8,128)S(1)}, u32[]{:S(2)}) copy-start(f32[256,1]{1,0:T(8,128)S(1)} %copy.176.refs_1_) | copy-start | bytes 3076
  142.0 3.7 copy-start.1
  160.4 0.9 copy-start.6
  161.3 0.9 copy-start.7
  162.2 0.9 copy-start.9
  163.0 0.8 copy-start.13
  163.8 0.7 copy-start.15
  164.6 0.7 copy-start.20
  167.3 1.7 copy-start.55
  169.8 41.1 %copy-start.26 = (f32[504,256]{1,0:T(8,128)S(1)}, f32[504,256]{1,0:T(8,128)}, u32[]{:S(2)}) copy-start(f32[504,256]{1,0:T(8,128)} %copy-done.25) | copy-start | bytes 1548292
  214.4 5.3 %copy-start.4 = (f32[256,1]{1,0:T(8,128)S(1)}, f32[256,1]{1,0:T(8,128)}, u32[]{:S(2)}) copy-start(f32[256,1]{1,0:T(8,128)} %copy-done.3) | copy-start | bytes 3076
  214.4 5.3 %copy-start.8 = (f32[256,768]{1,0:T(8,128)S(1)}, f32[256,768]{1,0:T(8,128)}, u32[]{:S(2)}) copy-start(f32[256,768]{1,0:T(8,128)} %copy-done.7) | copy-start | bytes 2359300
  214.4 5.3 %copy-start.10 = (f32[256,768]{1,0:T(8,128)S(1)}, f32[256,768]{1,0:T(8,128)}, u32[]{:S(2)}) copy-start(f32[256,768]{1,0:T(8,128)} %copy-done.9) | copy-start | bytes 2359300
  214.4 5.3 %copy-start.11 = (f32[256,768]{1,0:T(8,128)S(1)}, f32[256,768]{1,0:T(8,128)}, u32[]{:S(2)}) copy-start(f32[256,768]{1,0:T(8,128)} %get-tuple-element.56.refs_0_) | copy-start | bytes 2359300
  214.4 5.3 %copy-start.18 = (f32[7,768]{1,0:T(8,128)S(1)}, f32[7,768]{1,0:T(8,128)}, u32[]{:S(2)}) copy-start(f32[7,768]{1,0:T(8,128)} %refs_3_.3) | copy-start | bytes 64516
  214.4 5.3 %copy-start.24 = (f32[8,768]{1,0:T(8,128)S(1)}, f32[8,768]{1,0:T(8,128)}, u32[]{:S(2)}) copy-start(f32[8,768]{1,0:T(8,128)} %get-tuple-element.63.refs_11_) | copy-start | bytes 73732
  217.2 2.5 copy-start.14
  217.2 2.5 copy-start.16
  217.2 2.5 copy-start.21
  241.8 0.9 copy-start.12
  242.7 0.6 copy-start.22
  246.3 2.2 copy-start.32
  246.4 2.1 copy-start.33
  246.4 2.1 copy-start.34
  246.4 2.1 copy-start.35
  408.8 83.7 %copy-start.28 = (f32[3,2,96,768]{3,2,1,0:T(8,128)S(1)}, f32[3,2,96,768]{3,2,1,0:T(8,128)}, u32[]{:S(2)}) copy-start(f32[3,2,96,768]{3,2,1,0:T(8,128)} %param.45) | copy-start | bytes 5308420
  492.6 2.8 copy-start.30
  492.6 2.8 copy-start.36
  492.6 2.8 copy-start.38
  495.3 1.5 copy-start.40
  495.4 1.9 copy-start.44
  495.4 1.9 copy-start.51
  495.4 1.9 copy-start.52
  495.4 2.6 copy-start.47
  495.4 2.7 copy-start.48
  495.4 2.7 copy-start.42
  495.4 5.0 copy-start.37
  502.1 1.1 copy-start.31
  503.2 3.3 copy-start.43
  503.2 3.3 copy-start.49
  503.2 3.3 copy-start.50
  503.2 4.0 copy-start.41
  503.2 4.0 copy-start.39
  503.2 4.0 copy-start.45
  503.2 4.0 copy-start.46
  503.3 4.7 copy-start.53
  503.3 4.7 copy-start.54
